TPU v7x, 32 devices: a whole 2x2x4 slice. The times are simulated.
32 devices in a mesh: groups: 2 (over y), tensor: 4 (over z), dp: 4 (over x, core).
Axes of the slice: x: 2, y: 2, z: 4, core: 2. Of those that a mesh axis runs over, the one named last changes fastest.
Arguments:
- hidden: bfloat16 [2048, 53248], P(('groups', 'dp'), 'tensor'), parts along dimension 0, may hold values from -6 to 6
- down_weight: bfloat16 [53248, 8192], P('tensor', 'dp'), may hold values from -0.02734375 to 0.02734375
- scales: bfloat16 [8192], replicated, may hold values from 0.29882812 to 3
- residual: bfloat16 [2048, 8192], P('groups', ('dp', 'tensor')), parts along dimension 0, may hold values from -6 to 6
Outputs:
- updated: bfloat16 [2048, 8192], P('groups', ('dp', 'tensor')), parts along dimension 0
There are 2 independent parts, one for each index of `groups`. A program takes and returns all parts, laid end to end along the dimension named above; an argument that names none is the same for every part. Nothing has to cross between parts.
All inputs are finite; a program needn't handle non-finite values.
Results may differ from a plain program's by a relative error of at most 0.0046.
Values may be sent and summed in bfloat16 or wider, within the bound.
A program may use at most 256 MiB of HBM per device.

v0:
```python
import math

import jax
import jax.numpy as jnp
from jax import lax
from jax.experimental import pallas as pl
from jax.experimental.pallas import tpu as pltpu
from jax.sharding import PartitionSpec as P

LH = 64
WIDE = 256
CHUNKS = 4


def swap(x, axis, mask):
    return lax.ppermute(x, axis, [(i, i ^ mask) for i in range(lax.axis_size(axis))])


def sylvester(matrix_order):
    row_ids = lax.broadcasted_iota(jnp.int32, (matrix_order, matrix_order), 0)
    col_ids = lax.broadcasted_iota(jnp.int32, (matrix_order, matrix_order), 1)
    common_bits = row_ids & col_ids
    parity = jnp.zeros((matrix_order, matrix_order), jnp.int32)
    for bit_level in range(max(matrix_order.bit_length() - 1, 0)):
        parity = parity + (common_bits >> bit_level & 1)
    return jnp.where(parity % 2 == 0, 1.0, -1.0).astype(jnp.float32)


def any_size(hidden, down_weight, scales, residual):
    tensor_count = lax.axis_size("tensor")
    tok_rows, unit_count = hidden.shape
    local_table = sylvester(LH) / math.sqrt(LH)
    grouped = hidden.astype(jnp.float32).reshape(tok_rows, unit_count // LH, LH)
    current = jnp.einsum(
        "tbc,cd->tbd", grouped, local_table, precision=lax.Precision.HIGHEST
    ).reshape(tok_rows, unit_count)
    position = lax.axis_index("tensor")
    for bit_level in range(tensor_count.bit_length() - 1):
        partner = swap(current, "tensor", 1 << bit_level)
        upper_half = position >> bit_level & 1 == 1
        current = jnp.where(upper_half, partner - current, current + partner)
    rotated = (current * (1.0 / math.sqrt(tensor_count))).astype(jnp.bfloat16)
    out_cols = residual.shape[1]
    partial_cols = jnp.dot(
        lax.all_gather(rotated, "dp", axis=0, tiled=True),
        down_weight,
        preferred_element_type=jnp.float32,
    )
    owned_sums = lax.psum_scatter(partial_cols, "tensor", scatter_dimension=1, tiled=True)
    column = (lax.axis_index("dp") * tensor_count + position) * out_cols
    scale_cols = lax.dynamic_slice_in_dim(scales, column, out_cols).astype(jnp.float32)
    updated = residual.astype(jnp.float32) + scale_cols[None, :] * owned_sums
    return updated.astype(jnp.bfloat16)


def turn_kernel(own_table, table, a_ref, b_ref, r_ref, o_ref):
    for j in range(o_ref.shape[1] // WIDE):
        cols = slice(j * WIDE, (j + 1) * WIDE)
        acc = jnp.dot(a_ref[:, cols], own_table[...], preferred_element_type=jnp.float32)
        acc += jnp.dot(b_ref[:, cols], table[...], preferred_element_type=jnp.float32)
        acc += jnp.dot(r_ref[:, cols], table[...], preferred_element_type=jnp.float32)
        o_ref[:, cols] = acc.astype(o_ref.dtype)


def turn(own_table, table, a, b, r):
    rows, units = a.shape
    step = WIDE * next(n for n in (13, 8, 4, 2, 1) if units % (WIDE * n) == 0)
    whole = pl.BlockSpec((WIDE, WIDE), lambda i: (0, 0))
    part = pl.BlockSpec((rows, step), lambda i: (0, i))
    return pl.pallas_call(
        turn_kernel,
        grid=(units // step,),
        in_specs=[whole, whole, part, part, part],
        out_specs=part,
        out_shape=jax.ShapeDtypeStruct(a.shape, a.dtype),
        cost_estimate=pl.CostEstimate(
            flops=6 * rows * units * WIDE, bytes_accessed=8 * rows * units, transcendentals=0
        ),
    )(own_table, table, a, b, r)


def ring_of_four(hidden, down_weight, scales, residual):
    f32, bf16 = jnp.float32, jnp.bfloat16
    d = lax.axis_index("tensor")
    rank = lax.axis_index("dp")
    rows = hidden.shape[0]
    out_cols = residual.shape[1]
    odd = (d ^ d >> 1) & 1
    table = jnp.kron(jnp.eye(WIDE // LH, dtype=f32), sylvester(LH)) / 16.0
    own_sign = jnp.where(odd == 1, -1.0, 1.0)
    own_table = (table * own_sign).astype(bf16)
    table = table.astype(bf16)
    send_own = jnp.where(d >> 1 & 1 == 1, -1.0, 1.0)
    send_far = send_own * jnp.where(odd == 1, 1.0, -1.0)
    size = rows // CHUNKS

    def block(x, j):
        return lax.dynamic_slice_in_dim(x, j * out_cols, out_cols, 1)

    sums = []
    for k in range(CHUNKS):
        a = hidden[k * size : (k + 1) * size]
        b = swap(a, "tensor", 3)
        q = (send_own * a.astype(f32) + send_far * b.astype(f32)).astype(bf16)
        r = swap(q, "tensor", 1)
        rot = turn(own_table, table, a, b, r)
        far = swap(rot, "dp", 2)
        near = swap(rot, "dp", 1)
        both = swap(far, "dp", 1)
        tokens = jnp.concatenate([rot, near, far, both], axis=0)
        partial = jnp.dot(tokens, down_weight, preferred_element_type=f32)
        half = 2 * size
        done = []
        for rows_half, first, second in ((partial[:half], 3, 1), (partial[half:], 1, 3)):
            away = jnp.concatenate(
                [block(rows_half, d ^ first), block(rows_half, d ^ 2)], axis=1
            ).astype(bf16)
            back = swap(away, "tensor", first).astype(f32)
            onward = (block(rows_half, d ^ second) + back[:, out_cols:]).astype(bf16)
            last = swap(onward, "tensor", second).astype(f32)
            done.append(block(rows_half, d) + back[:, :out_cols] + last)
        sums.append(jnp.stack(done).reshape(4, size, out_cols))
    by_offset = jnp.concatenate(sums, axis=1)
    s0, s1, s2, s3 = by_offset
    low = rank & 1 == 1
    s0, s1 = jnp.where(low, s1, s0), jnp.where(low, s0, s1)
    s2, s3 = jnp.where(low, s3, s2), jnp.where(low, s2, s3)
    high = rank >> 1 & 1 == 1
    s0, s2 = jnp.where(high, s2, s0), jnp.where(high, s0, s2)
    s1, s3 = jnp.where(high, s3, s1), jnp.where(high, s1, s3)
    owned = jnp.concatenate([s0, s1, s2, s3], axis=0)
    column = (rank * 4 + d) * out_cols
    scale_cols = lax.dynamic_slice_in_dim(scales, column, out_cols).astype(f32)
    return (residual.astype(f32) + scale_cols[None, :] * owned).astype(bf16)


def shards(hidden, down_weight, scales, residual):
    fits = (
        lax.axis_size("tensor") == 4
        and lax.axis_size("dp") == 4
        and hidden.shape[0] % (16 * CHUNKS) == 0
        and hidden.shape[1] % WIDE == 0
    )
    return (ring_of_four if fits else any_size)(hidden, down_weight, scales, residual)


def solution(mesh):
    return jax.shard_map(
        shards,
        mesh=mesh,
        in_specs=(
            P(("groups", "dp"), "tensor"),
            P("tensor", "dp"),
            P(),
            P("groups", ("dp", "tensor")),
        ),
        out_specs=P("groups", ("dp", "tensor")),
        check_vma=False,
    )
```

profile of v0, /device:TPU:0, one launch (start us, length us, event | category | flops | bytes accessed | tf_op | source)
XLA Modules:
  0.0 674.9 jit_solution(10009017539642698713)
XLA Ops:
  0.0 5.9 fusion.68
  5.9 5.0 collective-permute-start
  11.0 3.8 collective-permute-start.27
  14.8 34.6 %collective-permute-done.b_ref = bf16[64,13312]{1,0:T(8,128)(2,1)} collective-permute-done((bf16[64,13312]{1,0:T(8,128)(2,1)}, bf16[64,13312]{1,0:T(8,128)(2,1)}, u32[]{:S(2)}, u32[]{:S(2)}) %collective-permute-start) | collective-permute-done | bytes 1703968 | tf_op jit(solution)/shard_map/ppermute | solution.py:16
  49.4 36.4 %collective-permute-done.18.b_ref = bf16[64,13312]{1,0:T(8,128)(2,1)S(1)} collective-permute-done((bf16[64,13312]{1,0:T(8,128)(2,1)}, bf16[64,13312]{1,0:T(8,128)(2,1)S(1)}, u32[]{:S(2)}, u32[]{:S(2)}) %collective-permute-start.18) | collective-permute-done | bytes 1703968 | tf_op jit(solution)/shard_map/ppermute | solution.py:16
  85.8 36.5 %collective-permute-done.27.b_ref = bf16[64,13312]{1,0:T(8,128)(2,1)S(1)} collective-permute-done((bf16[64,13312]{1,0:T(8,128)(2,1)}, bf16[64,13312]{1,0:T(8,128)(2,1)S(1)}, u32[]{:S(2)}, u32[]{:S(2)}) %collective-permute-start.27) | collective-permute-done | bytes 1703968 | tf_op jit(solution)/shard_map/ppermute | solution.py:16
  122.3 35.8 %collective-permute-done.9.b_ref = bf16[64,13312]{1,0:T(8,128)(2,1)} collective-permute-done((bf16[64,13312]{1,0:T(8,128)(2,1)}, bf16[64,13312]{1,0:T(8,128)(2,1)}, u32[]{:S(2)}, u32[]{:S(2)}) %collective-permute-start.9) | collective-permute-done | bytes 1703968 | tf_op jit(solution)/shard_map/ppermute | solution.py:16
  158.1 6.9 %add_convert_fusion.3 = (bf16[64,13312]{1,0:T(8,128)(2,1)}, bf16[64,13312]{1,0:T(8,128)(2,1)}, bf16[64,13312]{1,0:T(8,128)(2,1)}, bf16[64,13312]{1,0:T(8,128)(2,1)}) fusion(bf16[64,13312]{1,0:T(8,128)(2,1)} %collective-permute-done.b_ref, f32[]{:T(128)S(6)} %mul.159, f32[]{:T(128)S(6)} %select_n.148, bf16[256,13312]{1,0:T(8,128)(2,1)} %param.4, ...), kind=kLoop, calls=%fused_computation.35 | loop fusion | flops 20447232 | bytes 20447240 | tf_op jit(solution)/shard_map/convert_element_type | solution.py:104
  165.0 145.7 %collective-permute-start.1 = (bf16[64,13312]{1,0:T(8,128)(2,1)}, bf16[64,13312]{1,0:T(8,128)(2,1)}, u32[]{:S(2)}, u32[]{:S(2)}) collective-permute-start(bf16[64,13312]{1,0:T(8,128)(2,1)} %get-tuple-element.5), channel_id=1, source_target_pairs={{0,4},{4,0},{8,12},{12,8},{1,5},{5,1},{9,13},{13,9},{2,6},{6,2},{1... | collective-permute-start | bytes 5111816 | tf_op jit(solution)/shard_map/ppermute | solution.py:16
  311.1 0.9 convert_element_type.166.own_table
  312.0 0.8 convert_element_type.168.table
  312.8 36.4 %collective-permute-done.1.r_ref = bf16[64,13312]{1,0:T(8,128)(2,1)} collective-permute-done((bf16[64,13312]{1,0:T(8,128)(2,1)}, bf16[64,13312]{1,0:T(8,128)(2,1)}, u32[]{:S(2)}, u32[]{:S(2)}) %collective-permute-start.1) | collective-permute-done | bytes 1703968 | tf_op jit(solution)/shard_map/ppermute | solution.py:16
  349.2 6.8 %shard_map.46 = bf16[64,13312]{1,0:T(8,128)(2,1)} custom-call(bf16[256,256]{1,0:T(8,128)(2,1)} %convert_element_type.166.own_table, bf16[256,256]{1,0:T(8,128)(2,1)} %convert_element_type.168.table, bf16[64,13312]{1,0:T(8,128)(2,1)} %get-tuple-element.9.a_ref, bf16[64,13312]{1,0:T(8,128)(2,1)} %collective-permute-done.b_ref, ...), custom_call_target="tpu_custom_call" | custom-call | flops 1308622848 | bytes 6815744 | tf_op jit(solution)/shard_map/pallas_call | solution.py:70
  356.0 1.5 collective-permute-start.3
  357.5 2.0 collective-permute-start.19
  359.6 26.1 %collective-permute-done.10.r_ref = bf16[64,13312]{1,0:T(8,128)(2,1)} collective-permute-done((bf16[64,13312]{1,0:T(8,128)(2,1)}, bf16[64,13312]{1,0:T(8,128)(2,1)}, u32[]{:S(2)}, u32[]{:S(2)}) %collective-permute-start.10) | collective-permute-done | bytes 1703968 | tf_op jit(solution)/shard_map/ppermute | solution.py:16
  385.7 6.8 %shard_map.47 = bf16[64,13312]{1,0:T(8,128)(2,1)} custom-call(bf16[256,256]{1,0:T(8,128)(2,1)} %convert_element_type.166.own_table, bf16[256,256]{1,0:T(8,128)(2,1)} %convert_element_type.168.table, bf16[64,13312]{1,0:T(8,128)(2,1)} %get-tuple-element.10.a_ref, bf16[64,13312]{1,0:T(8,128)(2,1)} %collective-permute-done.9.b_ref, ...), custom_call_target="tpu_custom_call" | custom-call | flops 1308622848 | bytes 6815744 | tf_op jit(solution)/shard_map/pallas_call | solution.py:70
  392.5 1.5 collective-permute-start.12
  394.0 0.8 dynamic-slice_convert_fusion.16
  394.8 27.4 %collective-permute-done.19.r_ref = bf16[64,13312]{1,0:T(8,128)(2,1)} collective-permute-done((bf16[64,13312]{1,0:T(8,128)(2,1)S(1)}, bf16[64,13312]{1,0:T(8,128)(2,1)}, u32[]{:S(2)}, u32[]{:S(2)}) %collective-permute-start.19) | collective-permute-done | bytes 1703968 | tf_op jit(solution)/shard_map/ppermute | solution.py:16
  422.2 6.8 %shard_map.48 = bf16[64,13312]{1,0:T(8,128)(2,1)} custom-call(bf16[256,256]{1,0:T(8,128)(2,1)} %convert_element_type.166.own_table, bf16[256,256]{1,0:T(8,128)(2,1)} %convert_element_type.168.table, bf16[64,13312]{1,0:T(8,128)(2,1)} %get-tuple-element.12.a_ref, bf16[64,13312]{1,0:T(8,128)(2,1)} %copy-done.1, bf16[64,13312]{1,0:T(8,128)(2,1)} %collective-permute-done.19.r_ref), custom_call_target="tpu_custom_call" | custom-call | flops 1308622848 | bytes 6815744 | tf_op jit(solution)/shard_map/pallas_call | solution.py:70
  429.1 28.1 %collective-permute-done.28.r_ref = bf16[64,13312]{1,0:T(8,128)(2,1)} collective-permute-done((bf16[64,13312]{1,0:T(8,128)(2,1)S(1)}, bf16[64,13312]{1,0:T(8,128)(2,1)}, u32[]{:S(2)}, u32[]{:S(2)}) %collective-permute-start.28) | collective-permute-done | bytes 1703968 | tf_op jit(solution)/shard_map/ppermute | solution.py:16
  457.1 1.5 collective-permute-start.21
  458.6 6.8 %shard_map.49 = bf16[64,13312]{1,0:T(8,128)(2,1)} custom-call(bf16[256,256]{1,0:T(8,128)(2,1)} %convert_element_type.166.own_table, bf16[256,256]{1,0:T(8,128)(2,1)} %convert_element_type.168.table, bf16[64,13312]{1,0:T(8,128)(2,1)} %get-tuple-element.11.a_ref, bf16[64,13312]{1,0:T(8,128)(2,1)} %copy-done, bf16[64,13312]{1,0:T(8,128)(2,1)} %collective-permute-done.28.r_ref), custom_call_target="tpu_custom_call" | custom-call | flops 1308622848 | bytes 6815744 | tf_op jit(solution)/shard_map/pallas_call | solution.py:70
  466.3 24.0 %fusion = f32[256,2048]{1,0:T(8,128)S(1)} fusion(bf16[13312,2048]{1,0:T(8,128)(2,1)} %param.5, bf16[64,13312]{1,0:T(8,128)(2,1)} %collective-permute-done.4, bf16[64,13312]{1,0:T(8,128)(2,1)} %collective-permute-done.3, bf16[64,13312]{1,0:T(8,128)(2,1)} %collective-permute-done.2, bf16[64,13312]{1,0:T(8,128)(2,1)} %shard_map.46), kind=kOutput, calls=%fused_computation | convolution fusion | flops 13985906688 | bytes 63438848 | tf_op jit(solution)/shard_map/dot_general | solution.py:111
  490.7 6.9 %collective-permute-done.21 = bf16[64,13312]{1,0:T(8,128)(2,1)} collective-permute-done((bf16[64,13312]{1,0:T(8,128)(2,1)}, bf16[64,13312]{1,0:T(8,128)(2,1)}, u32[]{:S(2)}, u32[]{:S(2)}) %collective-permute-start.21) | collective-permute-done | bytes 1703968 | tf_op jit(solution)/shard_map/ppermute | solution.py:16
  497.6 34.0 %collective-permute-done.30 = bf16[64,13312]{1,0:T(8,128)(2,1)} collective-permute-done((bf16[64,13312]{1,0:T(8,128)(2,1)}, bf16[64,13312]{1,0:T(8,128)(2,1)}, u32[]{:S(2)}, u32[]{:S(2)}) %collective-permute-start.30) | collective-permute-done | bytes 1703968 | tf_op jit(solution)/shard_map/ppermute | solution.py:16
  531.6 25.5 %fusion.8 = f32[256,2048]{1,0:T(8,128)} fusion(bf16[13312,2048]{1,0:T(8,128)(2,1)} %param.5, bf16[64,13312]{1,0:T(8,128)(2,1)} %collective-permute-done.13, bf16[64,13312]{1,0:T(8,128)(2,1)} %collective-permute-done.12, bf16[64,13312]{1,0:T(8,128)(2,1)} %collective-permute-done.11, bf16[64,13312]{1,0:T(8,128)(2,1)} %shard_map.47), kind=kOutput, calls=%fused_computation.8 | convolution fusion | flops 13985906688 | bytes 63438848 | tf_op jit(solution)/shard_map/dot_general | solution.py:111
  557.3 1.4 copy-done.6
  558.9 0.7 copy-done.2
  559.7 0.8 pad_maximum_fusion.5
  560.4 2.1 collective-permute-start.5
  564.6 1.7 collective-permute-start.14
  566.3 25.3 %fusion.16 = f32[256,2048]{1,0:T(8,128)} fusion(bf16[13312,2048]{1,0:T(8,128)(2,1)} %param.5, bf16[64,13312]{1,0:T(8,128)(2,1)} %collective-permute-done.22, bf16[64,13312]{1,0:T(8,128)(2,1)} %collective-permute-done.21, bf16[64,13312]{1,0:T(8,128)(2,1)} %collective-permute-done.20, bf16[64,13312]{1,0:T(8,128)(2,1)} %shard_map.48), kind=kOutput, calls=%fused_computation.16 | convolution fusion | flops 13985906688 | bytes 63438848 | tf_op jit(solution)/shard_map/dot_general | solution.py:111
  591.6 0.7 pad_maximum_fusion.8
  592.3 3.1 fusion.71
  596.0 25.3 %fusion.24 = f32[256,2048]{1,0:T(8,128)} fusion(bf16[13312,2048]{1,0:T(8,128)(2,1)} %param.5, bf16[64,13312]{1,0:T(8,128)(2,1)} %collective-permute-done.31, bf16[64,13312]{1,0:T(8,128)(2,1)} %collective-permute-done.30, bf16[64,13312]{1,0:T(8,128)(2,1)} %collective-permute-done.29, bf16[64,13312]{1,0:T(8,128)(2,1)} %shard_map.49), kind=kOutput, calls=%fused_computation.24 | convolution fusion | flops 13985906688 | bytes 63438848 | tf_op jit(solution)/shard_map/dot_general | solution.py:111
  621.3 1.8 fusion.72
  623.3 2.2 collective-permute-start.23
  626.3 1.0 convert_element_type.172
  627.3 1.8 collective-permute-start.32
  629.1 1.0 convert_element_type.175
  630.8 1.0 convert_element_type.181
  631.9 1.5 collective-permute-start.6
  633.5 1.0 collective-permute-done.23
  634.5 2.1 collective-permute-start.8
  636.6 3.6 collective-permute-done.25
  640.2 4.0 collective-permute-start.15
  644.3 1.4 collective-permute-done.32
  645.7 2.1 collective-permute-start.17
  647.9 1.7 collective-permute-done.34
  649.6 2.0 collective-permute-start.24
  651.7 2.1 collective-permute-done.6
  653.8 2.1 collective-permute-start.26
  656.0 1.2 collective-permute-done.8
  657.2 2.3 collective-permute-done.15
  659.5 2.1 collective-permute-start.35
  661.6 1.2 collective-permute-done.17
  662.8 2.3 collective-permute-done.24
  665.1 3.2 collective-permute-done.26
  668.5 2.1 collective-permute-done.33
  670.8 1.3 collective-permute-done.35
  672.8 0.9 copy-done.9
  673.6 1.3 fusion.33
  (91 shorter events, 8.1 us)
Async XLA Ops:
  5.9 43.5 %collective-permute-start = (bf16[64,13312]{1,0:T(8,128)(2,1)}, bf16[64,13312]{1,0:T(8,128)(2,1)}, u32[]{:S(2)}, u32[]{:S(2)}) collective-permute-start(bf16[64,13312]{1,0:T(8,128)(2,1)} %get-tuple-element.9.a_ref), channel_id=1, source_target_pairs={{0,12},{4,8},{8,4},{12,0},{1,13},{5,9},{9,5},{13,1},{2,14},{6,10},... | collective-permute-start | bytes 5111816 | tf_op jit(solution)/shard_map/ppermute | solution.py:16
  10.9 74.9 %collective-permute-start.18 = (bf16[64,13312]{1,0:T(8,128)(2,1)}, bf16[64,13312]{1,0:T(8,128)(2,1)S(1)}, u32[]{:S(2)}, u32[]{:S(2)}) collective-permute-start(bf16[64,13312]{1,0:T(8,128)(2,1)} %get-tuple-element.12.a_ref), channel_id=1, source_target_pairs={{0,12},{4,8},{8,4},{12,0},{1,13},{5,9},{9,5},{13,1},{2,14},{6,10},... | collective-permute-start | bytes 5111816 | tf_op jit(solution)/shard_map/ppermute | solution.py:16
  11.0 111.3 %collective-permute-start.27 = (bf16[64,13312]{1,0:T(8,128)(2,1)}, bf16[64,13312]{1,0:T(8,128)(2,1)S(1)}, u32[]{:S(2)}, u32[]{:S(2)}) collective-permute-start(bf16[64,13312]{1,0:T(8,128)(2,1)} %get-tuple-element.11.a_ref), channel_id=1, source_target_pairs={{0,12},{4,8},{8,4},{12,0},{1,13},{5,9},{9,5},{13,1},{2,14},{6,10},... | collective-permute-start | bytes 5111816 | tf_op jit(solution)/shard_map/ppermute | solution.py:16
  14.8 143.3 %collective-permute-start.9 = (bf16[64,13312]{1,0:T(8,128)(2,1)}, bf16[64,13312]{1,0:T(8,128)(2,1)}, u32[]{:S(2)}, u32[]{:S(2)}) collective-permute-start(bf16[64,13312]{1,0:T(8,128)(2,1)} %get-tuple-element.10.a_ref), channel_id=1, source_target_pairs={{0,12},{4,8},{8,4},{12,0},{1,13},{5,9},{9,5},{13,1},{2,14},{6,10},... | collective-permute-start | bytes 5111816 | tf_op jit(solution)/shard_map/ppermute | solution.py:16
  85.8 79.2 %copy-start.1 = (bf16[64,13312]{1,0:T(8,128)(2,1)}, bf16[64,13312]{1,0:T(8,128)(2,1)S(1)}, u32[]{:S(2)}) copy-start(bf16[64,13312]{1,0:T(8,128)(2,1)S(1)} %collective-permute-done.18.b_ref) | copy-start | bytes 5111812
  122.3 42.7 %copy-start = (bf16[64,13312]{1,0:T(8,128)(2,1)}, bf16[64,13312]{1,0:T(8,128)(2,1)S(1)}, u32[]{:S(2)}) copy-start(bf16[64,13312]{1,0:T(8,128)(2,1)S(1)} %collective-permute-done.27.b_ref) | copy-start | bytes 5111812
  165.0 184.2 %collective-permute-start.1 = (bf16[64,13312]{1,0:T(8,128)(2,1)}, bf16[64,13312]{1,0:T(8,128)(2,1)}, u32[]{:S(2)}, u32[]{:S(2)}) collective-permute-start(bf16[64,13312]{1,0:T(8,128)(2,1)} %get-tuple-element.5), channel_id=1, source_target_pairs={{0,4},{4,0},{8,12},{12,8},{1,5},{5,1},{9,13},{13,9},{2,6},{6,2},{1... | collective-permute-start | bytes 5111816 | tf_op jit(solution)/shard_map/ppermute | solution.py:16
  312.0 73.8 %collective-permute-start.10 = (bf16[64,13312]{1,0:T(8,128)(2,1)}, bf16[64,13312]{1,0:T(8,128)(2,1)}, u32[]{:S(2)}, u32[]{:S(2)}) collective-permute-start(bf16[64,13312]{1,0:T(8,128)(2,1)} %get-tuple-element.6), channel_id=1, source_target_pairs={{0,4},{4,0},{8,12},{12,8},{1,5},{5,1},{9,13},{13,9},{2,6},{6,2},{1... | collective-permute-start | bytes 5111816 | tf_op jit(solution)/shard_map/ppermute | solution.py:16
  312.8 44.7 %copy-start.8 = (bf16[64,13312]{1,0:T(8,128)(2,1)S(1)}, bf16[64,13312]{1,0:T(8,128)(2,1)}, u32[]{:S(2)}) copy-start(bf16[64,13312]{1,0:T(8,128)(2,1)} %get-tuple-element.7) | copy-start | bytes 5111812
  312.8 46.7 %copy-start.7 = (bf16[64,13312]{1,0:T(8,128)(2,1)S(1)}, bf16[64,13312]{1,0:T(8,128)(2,1)}, u32[]{:S(2)}) copy-start(bf16[64,13312]{1,0:T(8,128)(2,1)} %get-tuple-element.8) | copy-start | bytes 5111812
  356.0 38.0 %collective-permute-start.3 = (bf16[64,13312]{1,0:T(8,128)(2,1)}, bf16[64,13312]{1,0:T(8,128)(2,1)}, u32[]{:S(2)}, u32[]{:S(2)}) collective-permute-start(bf16[64,13312]{1,0:T(8,128)(2,1)} %shard_map.46), channel_id=1, source_target_pairs={{0,2},{1,3},{2,0},{3,1},{4,6},{5,7},{6,4},{7,5},{8,10},{9,11},{10,... | collective-permute-start | bytes 5111816 | tf_op jit(solution)/shard_map/ppermute | solution.py:16
  357.5 64.7 %collective-permute-start.19 = (bf16[64,13312]{1,0:T(8,128)(2,1)S(1)}, bf16[64,13312]{1,0:T(8,128)(2,1)}, u32[]{:S(2)}, u32[]{:S(2)}) collective-permute-start(bf16[64,13312]{1,0:T(8,128)(2,1)S(1)} %copy-done.8), channel_id=1, source_target_pairs={{0,4},{4,0},{8,12},{12,8},{1,5},{5,1},{9,13},{13,9},{2,6},{6,2},{1... | collective-permute-start | bytes 5111816 | tf_op jit(solution)/shard_map/ppermute | solution.py:16
  359.6 97.6 %collective-permute-start.28 = (bf16[64,13312]{1,0:T(8,128)(2,1)S(1)}, bf16[64,13312]{1,0:T(8,128)(2,1)}, u32[]{:S(2)}, u32[]{:S(2)}) collective-permute-start(bf16[64,13312]{1,0:T(8,128)(2,1)S(1)} %copy-done.7), channel_id=1, source_target_pairs={{0,4},{4,0},{8,12},{12,8},{1,5},{5,1},{9,13},{13,9},{2,6},{6,2},{1... | collective-permute-start | bytes 5111816 | tf_op jit(solution)/shard_map/ppermute | solution.py:16
  359.6 105.8 %collective-permute-start.2 = (bf16[64,13312]{1,0:T(8,128)(2,1)}, bf16[64,13312]{1,0:T(8,128)(2,1)}, u32[]{:S(2)}, u32[]{:S(2)}) collective-permute-start(bf16[64,13312]{1,0:T(8,128)(2,1)} %shard_map.46), channel_id=1, source_target_pairs={{0,1},{1,0},{2,3},{3,2},{4,5},{5,4},{6,7},{7,6},{8,9},{9,8},{10,11... | collective-permute-start | bytes 5111816 | tf_op jit(solution)/shard_map/ppermute | solution.py:16
  392.5 72.9 %collective-permute-start.12 = (bf16[64,13312]{1,0:T(8,128)(2,1)}, bf16[64,13312]{1,0:T(8,128)(2,1)}, u32[]{:S(2)}, u32[]{:S(2)}) collective-permute-start(bf16[64,13312]{1,0:T(8,128)(2,1)} %shard_map.47), channel_id=1, source_target_pairs={{0,2},{1,3},{2,0},{3,1},{4,6},{5,7},{6,4},{7,5},{8,10},{9,11},{10,... | collective-permute-start | bytes 5111816 | tf_op jit(solution)/shard_map/ppermute | solution.py:16
  394.0 72.1 %collective-permute-start.4 = (bf16[64,13312]{1,0:T(8,128)(2,1)}, bf16[64,13312]{1,0:T(8,128)(2,1)}, u32[]{:S(2)}, u32[]{:S(2)}) collective-permute-start(bf16[64,13312]{1,0:T(8,128)(2,1)} %collective-permute-done.3), channel_id=1, source_target_pairs={{0,1},{1,0},{2,3},{3,2},{4,5},{5,4},{6,7},{7,6},{8,9},{9,8},{10,11... | collective-permute-start | bytes 5111816 | tf_op jit(solution)/shard_map/ppermute | solution.py:16
  422.2 68.0 %collective-permute-start.11 = (bf16[64,13312]{1,0:T(8,128)(2,1)}, bf16[64,13312]{1,0:T(8,128)(2,1)}, u32[]{:S(2)}, u32[]{:S(2)}) collective-permute-start(bf16[64,13312]{1,0:T(8,128)(2,1)} %shard_map.47), channel_id=1, source_target_pairs={{0,1},{1,0},{2,3},{3,2},{4,5},{5,4},{6,7},{7,6},{8,9},{9,8},{10,11... | collective-permute-start | bytes 5111816 | tf_op jit(solution)/shard_map/ppermute | solution.py:16
  457.1 40.5 %collective-permute-start.21 = (bf16[64,13312]{1,0:T(8,128)(2,1)}, bf16[64,13312]{1,0:T(8,128)(2,1)}, u32[]{:S(2)}, u32[]{:S(2)}) collective-permute-start(bf16[64,13312]{1,0:T(8,128)(2,1)} %shard_map.48), channel_id=1, source_target_pairs={{0,2},{1,3},{2,0},{3,1},{4,6},{5,7},{6,4},{7,5},{8,10},{9,11},{10,... | collective-permute-start | bytes 5111816 | tf_op jit(solution)/shard_map/ppermute | solution.py:16
  465.5 98.6 %collective-permute-start.20 = (bf16[64,13312]{1,0:T(8,128)(2,1)}, bf16[64,13312]{1,0:T(8,128)(2,1)}, u32[]{:S(2)}, u32[]{:S(2)}) collective-permute-start(bf16[64,13312]{1,0:T(8,128)(2,1)} %shard_map.48), channel_id=1, source_target_pairs={{0,1},{1,0},{2,3},{3,2},{4,5},{5,4},{6,7},{7,6},{8,9},{9,8},{10,11... | collective-permute-start | bytes 5111816 | tf_op jit(solution)/shard_map/ppermute | solution.py:16
  465.5 66.1 %collective-permute-start.30 = (bf16[64,13312]{1,0:T(8,128)(2,1)}, bf16[64,13312]{1,0:T(8,128)(2,1)}, u32[]{:S(2)}, u32[]{:S(2)}) collective-permute-start(bf16[64,13312]{1,0:T(8,128)(2,1)} %shard_map.49), channel_id=1, source_target_pairs={{0,2},{1,3},{2,0},{3,1},{4,6},{5,7},{6,4},{7,5},{8,10},{9,11},{10,... | collective-permute-start | bytes 5111816 | tf_op jit(solution)/shard_map/ppermute | solution.py:16
  466.1 65.5 %collective-permute-start.13 = (bf16[64,13312]{1,0:T(8,128)(2,1)}, bf16[64,13312]{1,0:T(8,128)(2,1)}, u32[]{:S(2)}, u32[]{:S(2)}) collective-permute-start(bf16[64,13312]{1,0:T(8,128)(2,1)} %collective-permute-done.12), channel_id=1, source_target_pairs={{0,1},{1,0},{2,3},{3,2},{4,5},{5,4},{6,7},{7,6},{8,9},{9,8},{10,11... | collective-permute-start | bytes 5111816 | tf_op jit(solution)/shard_map/ppermute | solution.py:16
  490.3 105.2 %collective-permute-start.29 = (bf16[64,13312]{1,0:T(8,128)(2,1)}, bf16[64,13312]{1,0:T(8,128)(2,1)}, u32[]{:S(2)}, u32[]{:S(2)}) collective-permute-start(bf16[64,13312]{1,0:T(8,128)(2,1)} %shard_map.49), channel_id=1, source_target_pairs={{0,1},{1,0},{2,3},{3,2},{4,5},{5,4},{6,7},{7,6},{8,9},{9,8},{10,11... | collective-permute-start | bytes 5111816 | tf_op jit(solution)/shard_map/ppermute | solution.py:16
  497.6 67.0 %collective-permute-start.22 = (bf16[64,13312]{1,0:T(8,128)(2,1)}, bf16[64,13312]{1,0:T(8,128)(2,1)}, u32[]{:S(2)}, u32[]{:S(2)}) collective-permute-start(bf16[64,13312]{1,0:T(8,128)(2,1)} %collective-permute-done.21), channel_id=1, source_target_pairs={{0,1},{1,0},{2,3},{3,2},{4,5},{5,4},{6,7},{7,6},{8,9},{9,8},{10,11... | collective-permute-start | bytes 5111816 | tf_op jit(solution)/shard_map/ppermute | solution.py:16
  531.6 64.4 %collective-permute-start.31 = (bf16[64,13312]{1,0:T(8,128)(2,1)}, bf16[64,13312]{1,0:T(8,128)(2,1)}, u32[]{:S(2)}, u32[]{:S(2)}) collective-permute-start(bf16[64,13312]{1,0:T(8,128)(2,1)} %collective-permute-done.30), channel_id=1, source_target_pairs={{0,1},{1,0},{2,3},{3,2},{4,5},{5,4},{6,7},{7,6},{8,9},{9,8},{10,11... | collective-permute-start | bytes 5111816 | tf_op jit(solution)/shard_map/ppermute | solution.py:16
  557.1 1.6 copy-start.6
  558.6 1.0 copy-start.2
  560.4 65.2 %collective-permute-start.5 = (bf16[128,1024]{1,0:T(8,128)(2,1)}, bf16[128,1024]{1,0:T(8,128)(2,1)}, u32[]{:S(2)}, u32[]{:S(2)}) collective-permute-start(bf16[128,1024]{1,0:T(8,128)(2,1)} %pad_maximum_fusion.5), channel_id=1, source_target_pairs={{0,12},{4,8},{8,4},{12,0},{1,13},{5,9},{9,5},{13,1},{2,14},{6,10},... | collective-permute-start | bytes 786440 | tf_op jit(solution)/shard_map/ppermute | solution.py:16
  564.1 63.3 %collective-permute-start.7 = (bf16[128,1024]{1,0:T(8,128)(2,1)}, bf16[128,1024]{1,0:T(8,128)(2,1)}, u32[]{:S(2)}, u32[]{:S(2)}) collective-permute-start(bf16[128,1024]{1,0:T(8,128)(2,1)} %pad_maximum_fusion.6), channel_id=1, source_target_pairs={{0,4},{4,0},{8,12},{12,8},{1,5},{5,1},{9,13},{13,9},{2,6},{6,2},{1... | collective-permute-start | bytes 786440 | tf_op jit(solution)/shard_map/ppermute | solution.py:16
  564.6 65.5 %collective-permute-start.14 = (bf16[128,1024]{1,0:T(8,128)(2,1)}, bf16[128,1024]{1,0:T(8,128)(2,1)}, u32[]{:S(2)}, u32[]{:S(2)}) collective-permute-start(bf16[128,1024]{1,0:T(8,128)(2,1)} %pad_maximum_fusion.7), channel_id=1, source_target_pairs={{0,12},{4,8},{8,4},{12,0},{1,13},{5,9},{9,5},{13,1},{2,14},{6,10},... | collective-permute-start | bytes 786440 | tf_op jit(solution)/shard_map/ppermute | solution.py:16
  595.4 36.4 %collective-permute-start.16 = (bf16[128,1024]{1,0:T(8,128)(2,1)}, bf16[128,1024]{1,0:T(8,128)(2,1)S(1)}, u32[]{:S(2)}, u32[]{:S(2)}) collective-permute-start(bf16[128,1024]{1,0:T(8,128)(2,1)} %pad_maximum_fusion.8), channel_id=1, source_target_pairs={{0,4},{4,0},{8,12},{12,8},{1,5},{5,1},{9,13},{13,9},{2,6},{6,2},{1... | collective-permute-start | bytes 786440 | tf_op jit(solution)/shard_map/ppermute | solution.py:16
  621.3 1.9 copy-start.5
  621.3 4.1 copy-start.4
  623.3 4.0 copy-start.3
  623.3 11.1 %collective-permute-start.23 = (bf16[128,1024]{1,0:T(8,128)(2,1)S(1)}, bf16[128,1024]{1,0:T(8,128)(2,1)S(1)}, u32[]{:S(2)}, u32[]{:S(2)}) collective-permute-start(bf16[128,1024]{1,0:T(8,128)(2,1)S(1)} %pad_maximum_fusion.9), channel_id=1, source_target_pairs={{0,12},{4,8},{8,4},{12,0},{1,13},{5,9},{9,5},{13,1},{2,14},{6,10},... | collective-permute-start | bytes 786440 | tf_op jit(solution)/shard_map/ppermute | solution.py:16
  625.6 14.6 %collective-permute-start.25 = (bf16[128,1024]{1,0:T(8,128)(2,1)S(1)}, bf16[128,1024]{1,0:T(8,128)(2,1)S(1)}, u32[]{:S(2)}, u32[]{:S(2)}) collective-permute-start(bf16[128,1024]{1,0:T(8,128)(2,1)S(1)} %pad_maximum_fusion.10), channel_id=1, source_target_pairs={{0,4},{4,0},{8,12},{12,8},{1,5},{5,1},{9,13},{13,9},{2,6},{6,2},{1... | collective-permute-start | bytes 786440 | tf_op jit(solution)/shard_map/ppermute | solution.py:16
  627.3 18.4 %collective-permute-start.32 = (bf16[128,1024]{1,0:T(8,128)(2,1)S(1)}, bf16[128,1024]{1,0:T(8,128)(2,1)S(1)}, u32[]{:S(2)}, u32[]{:S(2)}) collective-permute-start(bf16[128,1024]{1,0:T(8,128)(2,1)S(1)} %pad_maximum_fusion.11), channel_id=1, source_target_pairs={{0,12},{4,8},{8,4},{12,0},{1,13},{5,9},{9,5},{13,1},{2,14},{6,10},... | collective-permute-start | bytes 786440 | tf_op jit(solution)/shard_map/ppermute | solution.py:16
  630.2 19.5 %collective-permute-start.34 = (bf16[128,1024]{1,0:T(8,128)(2,1)S(1)}, bf16[128,1024]{1,0:T(8,128)(2,1)S(1)}, u32[]{:S(2)}, u32[]{:S(2)}) collective-permute-start(bf16[128,1024]{1,0:T(8,128)(2,1)S(1)} %pad_maximum_fusion.12), channel_id=1, source_target_pairs={{0,4},{4,0},{8,12},{12,8},{1,5},{5,1},{9,13},{13,9},{2,6},{6,2},{1... | collective-permute-start | bytes 786440 | tf_op jit(solution)/shard_map/ppermute | solution.py:16
  631.9 22.0 %collective-permute-start.6 = (bf16[128,512]{1,0:T(8,128)(2,1)S(1)}, bf16[128,512]{1,0:T(8,128)(2,1)S(1)}, u32[]{:S(2)}, u32[]{:S(2)}) collective-permute-start(bf16[128,512]{1,0:T(8,128)(2,1)S(1)} %fusion.57), channel_id=1, source_target_pairs={{0,4},{4,0},{8,12},{12,8},{1,5},{5,1},{9,13},{13,9},{2,6},{6,2},{1... | collective-permute-start | bytes 393224 | tf_op jit(solution)/shard_map/ppermute | solution.py:16
  634.5 22.7 %collective-permute-start.8 = (bf16[128,512]{1,0:T(8,128)(2,1)S(1)}, bf16[128,512]{1,0:T(8,128)(2,1)S(1)}, u32[]{:S(2)}, u32[]{:S(2)}) collective-permute-start(bf16[128,512]{1,0:T(8,128)(2,1)S(1)} %fusion.54), channel_id=1, source_target_pairs={{0,12},{4,8},{8,4},{12,0},{1,13},{5,9},{9,5},{13,1},{2,14},{6,10},... | collective-permute-start | bytes 393224 | tf_op jit(solution)/shard_map/ppermute | solution.py:16
  640.2 19.2 %collective-permute-start.15 = (bf16[128,512]{1,0:T(8,128)(2,1)S(1)}, bf16[128,512]{1,0:T(8,128)(2,1)S(1)}, u32[]{:S(2)}, u32[]{:S(2)}) collective-permute-start(bf16[128,512]{1,0:T(8,128)(2,1)S(1)} %fusion.51), channel_id=1, source_target_pairs={{0,4},{4,0},{8,12},{12,8},{1,5},{5,1},{9,13},{13,9},{2,6},{6,2},{1... | collective-permute-start | bytes 393224 | tf_op jit(solution)/shard_map/ppermute | solution.py:16
  645.7 17.0 %collective-permute-start.17 = (bf16[128,512]{1,0:T(8,128)(2,1)S(1)}, bf16[128,512]{1,0:T(8,128)(2,1)S(1)}, u32[]{:S(2)}, u32[]{:S(2)}) collective-permute-start(bf16[128,512]{1,0:T(8,128)(2,1)S(1)} %fusion.48), channel_id=1, source_target_pairs={{0,12},{4,8},{8,4},{12,0},{1,13},{5,9},{9,5},{13,1},{2,14},{6,10},... | collective-permute-start | bytes 393224 | tf_op jit(solution)/shard_map/ppermute | solution.py:16
  649.6 15.4 %collective-permute-start.24 = (bf16[128,512]{1,0:T(8,128)(2,1)S(1)}, bf16[128,512]{1,0:T(8,128)(2,1)S(1)}, u32[]{:S(2)}, u32[]{:S(2)}) collective-permute-start(bf16[128,512]{1,0:T(8,128)(2,1)S(1)} %fusion.45), channel_id=1, source_target_pairs={{0,4},{4,0},{8,12},{12,8},{1,5},{5,1},{9,13},{13,9},{2,6},{6,2},{1... | collective-permute-start | bytes 393224 | tf_op jit(solution)/shard_map/ppermute | solution.py:16
  653.8 14.5 %collective-permute-start.26 = (bf16[128,512]{1,0:T(8,128)(2,1)S(1)}, bf16[128,512]{1,0:T(8,128)(2,1)S(1)}, u32[]{:S(2)}, u32[]{:S(2)}) collective-permute-start(bf16[128,512]{1,0:T(8,128)(2,1)S(1)} %fusion.42), channel_id=1, source_target_pairs={{0,12},{4,8},{8,4},{12,0},{1,13},{5,9},{9,5},{13,1},{2,14},{6,10},... | collective-permute-start | bytes 393224 | tf_op jit(solution)/shard_map/ppermute | solution.py:16
  657.1 13.5 %collective-permute-start.33 = (bf16[128,512]{1,0:T(8,128)(2,1)S(1)}, bf16[128,512]{1,0:T(8,128)(2,1)S(1)}, u32[]{:S(2)}, u32[]{:S(2)}) collective-permute-start(bf16[128,512]{1,0:T(8,128)(2,1)S(1)} %fusion.39), channel_id=1, source_target_pairs={{0,4},{4,0},{8,12},{12,8},{1,5},{5,1},{9,13},{13,9},{2,6},{6,2},{1... | collective-permute-start | bytes 393224 | tf_op jit(solution)/shard_map/ppermute | solution.py:16
  659.5 12.6 %collective-permute-start.35 = (bf16[128,512]{1,0:T(8,128)(2,1)S(1)}, bf16[128,512]{1,0:T(8,128)(2,1)S(1)}, u32[]{:S(2)}, u32[]{:S(2)}) collective-permute-start(bf16[128,512]{1,0:T(8,128)(2,1)S(1)} %fusion.36), channel_id=1, source_target_pairs={{0,12},{4,8},{8,4},{12,0},{1,13},{5,9},{9,5},{13,1},{2,14},{6,10},... | collective-permute-start | bytes 393224 | tf_op jit(solution)/shard_map/ppermute | solution.py:16
  672.4 1.2 copy-start.9
where the time goes:
time: 676 us; the launch traced here: 675 us
  waiting for transfers between devices  326 us (48%)
  starting transfers between devices  188 us (28%)
  matrix products  100 us (15%)
  Pallas kernels  27.3 us (4%)
  other arithmetic  17 us (3%)
  local copies, waits for them, and re-layouts  16.3 us (2%)
    ppermute x36, waiting for transfers between devices, swap(): lax.ppermute(x, axis, [(i, i ^ mask) for i in range(lax.axis_size(axis))])  326 us
    ppermute x36, starting transfers between devices, swap(): lax.ppermute(x, axis, [(i, i ^ mask) for i in range(lax.axis_size(axis))])  188 us
    dot_general x4, matrix products, ring_of_four(): partial = jnp.dot(tokens, down_weight, preferred_element_type=f32)  100 us
    pallas_call x4, Pallas kernels, turn(): pl.pallas_call(turn_kernel, grid=(units // step,), in_specs=[whole, whole...  27.3 us
  transfers between devices with their start and end apart: 36, of which 22 were waited for; matrix products, arithmetic and copies ran while one was open for 17% of the time, Pallas kernels for 4%

commit v1 on v0

--- a/solution.py
+++ b/solution.py
@@ -9,7 +9,9 @@
 
 LH = 64
 WIDE = 256
-CHUNKS = 4
+CHUNKS = (32, 32, 32, 32, 32, 32, 32, 16, 16)
+LAG = 2
+AHEAD = 2
 
 
 def swap(x, axis, mask):
@@ -53,73 +55,121 @@
     return updated.astype(jnp.bfloat16)
 
 
-def turn_kernel(own_table, table, a_ref, b_ref, r_ref, o_ref):
-    for j in range(o_ref.shape[1] // WIDE):
+def turn_kernel(signs, table, a_ref, near_ref, far_ref, last_ref, order_ref, own_ref, other_ref):
+    rows = a_ref.shape[0]
+    for j in range(a_ref.shape[1] // WIDE):
         cols = slice(j * WIDE, (j + 1) * WIDE)
-        acc = jnp.dot(a_ref[:, cols], own_table[...], preferred_element_type=jnp.float32)
-        acc += jnp.dot(b_ref[:, cols], table[...], preferred_element_type=jnp.float32)
-        acc += jnp.dot(r_ref[:, cols], table[...], preferred_element_type=jnp.float32)
-        o_ref[:, cols] = acc.astype(o_ref.dtype)
-
-
-def turn(own_table, table, a, b, r):
+        units = jnp.concatenate([ref[:, cols] for ref in (a_ref, near_ref, far_ref, last_ref)])
+        turned = jnp.dot(units, table[...], preferred_element_type=jnp.float32)
+        parts = [turned[i * rows : (i + 1) * rows] for i in range(4)]
+        for u, out in enumerate((own_ref, other_ref)):
+            total = signs[u, 0] * parts[0]
+            for i in range(1, 4):
+                total += signs[u, i] * parts[i]
+            out[:, cols] = total.astype(out.dtype)
+
+
+def turn(signs, table, a, near, far, last, order):
     rows, units = a.shape
     step = WIDE * next(n for n in (13, 8, 4, 2, 1) if units % (WIDE * n) == 0)
-    whole = pl.BlockSpec((WIDE, WIDE), lambda i: (0, 0))
     part = pl.BlockSpec((rows, step), lambda i: (0, i))
     return pl.pallas_call(
         turn_kernel,
         grid=(units // step,),
-        in_specs=[whole, whole, part, part, part],
-        out_specs=part,
-        out_shape=jax.ShapeDtypeStruct(a.shape, a.dtype),
+        in_specs=[
+            pl.BlockSpec(memory_space=pltpu.SMEM),
+            pl.BlockSpec((WIDE, WIDE), lambda i: (0, 0)),
+            part,
+            part,
+            part,
+            part,
+            pl.BlockSpec(memory_space=pl.ANY),
+        ],
+        out_specs=[part, part],
+        out_shape=[jax.ShapeDtypeStruct(a.shape, a.dtype)] * 2,
         cost_estimate=pl.CostEstimate(
-            flops=6 * rows * units * WIDE, bytes_accessed=8 * rows * units, transcendentals=0
+            flops=8 * rows * units * WIDE, bytes_accessed=12 * rows * units, transcendentals=0
         ),
-    )(own_table, table, a, b, r)
-
-
-def ring_of_four(hidden, down_weight, scales, residual):
+    )(signs, table, a, near, far, last, order)
+
+
+def down_kernel(t0, t1, t2, t3, weight_ref, order_ref, o_ref):
+    @pl.when(pl.program_id(0) == 0)
+    def _():
+        o_ref[...] = jnp.zeros_like(o_ref)
+
+    tokens = jnp.concatenate([t0[...], t1[...], t2[...], t3[...]])
+    o_ref[...] += jnp.dot(tokens, weight_ref[...], preferred_element_type=jnp.float32)
+
+
+def down(tokens, weight, order):
+    rows, units = tokens[0].shape
+    cols = weight.shape[1]
+    step = next(n for n in (1024, 512, 256) if units % n == 0)
+    part = pl.BlockSpec((rows, step), lambda i: (0, i))
+    return pl.pallas_call(
+        down_kernel,
+        grid=(units // step,),
+        in_specs=[part] * 4
+        + [pl.BlockSpec((step, cols), lambda i: (i, 0)), pl.BlockSpec(memory_space=pl.ANY)],
+        out_specs=pl.BlockSpec((4 * rows, cols), lambda i: (0, 0)),
+        out_shape=jax.ShapeDtypeStruct((4 * rows, cols), jnp.float32),
+        compiler_params=pltpu.CompilerParams(vmem_limit_bytes=32 * 1024 * 1024),
+        cost_estimate=pl.CostEstimate(
+            flops=8 * rows * units * cols, bytes_accessed=2 * units * cols, transcendentals=0
+        ),
+    )(*tokens, weight, order)
+
+
+def after(x, other):
+    return lax.optimization_barrier((x, other))[0]
+
+
+def line_of_four(hidden, down_weight, scales, residual):
     f32, bf16 = jnp.float32, jnp.bfloat16
     d = lax.axis_index("tensor")
     rank = lax.axis_index("dp")
-    rows = hidden.shape[0]
     out_cols = residual.shape[1]
-    odd = (d ^ d >> 1) & 1
-    table = jnp.kron(jnp.eye(WIDE // LH, dtype=f32), sylvester(LH)) / 16.0
-    own_sign = jnp.where(odd == 1, -1.0, 1.0)
-    own_table = (table * own_sign).astype(bf16)
-    table = table.astype(bf16)
-    send_own = jnp.where(d >> 1 & 1 == 1, -1.0, 1.0)
-    send_far = send_own * jnp.where(odd == 1, 1.0, -1.0)
-    size = rows // CHUNKS
+    inner = (d ^ d >> 1) & 1 == 1
+    table = (jnp.kron(jnp.eye(WIDE // LH, dtype=f32), sylvester(LH)) / 16.0).astype(bf16)
+
+    def sign(u, s):
+        both = u & s
+        return jnp.where((both ^ both >> 1) & 1 == 1, -1.0, 1.0).astype(f32)
+
+    signs = jnp.stack([jnp.stack([sign(u, d ^ m) for m in (0, 1, 3, 2)]) for u in (d, d ^ 1)])
+    inward, across, outward = [(0, 1), (3, 2)], [(1, 2), (2, 1)], [(1, 0), (2, 3)]
 
     def block(x, j):
         return lax.dynamic_slice_in_dim(x, j * out_cols, out_cols, 1)
 
-    sums = []
-    for k in range(CHUNKS):
-        a = hidden[k * size : (k + 1) * size]
-        b = swap(a, "tensor", 3)
-        q = (send_own * a.astype(f32) + send_far * b.astype(f32)).astype(bf16)
-        r = swap(q, "tensor", 1)
-        rot = turn(own_table, table, a, b, r)
-        far = swap(rot, "dp", 2)
-        near = swap(rot, "dp", 1)
-        both = swap(far, "dp", 1)
-        tokens = jnp.concatenate([rot, near, far, both], axis=0)
-        partial = jnp.dot(tokens, down_weight, preferred_element_type=f32)
-        half = 2 * size
-        done = []
-        for rows_half, first, second in ((partial[:half], 3, 1), (partial[half:], 1, 3)):
-            away = jnp.concatenate(
-                [block(rows_half, d ^ first), block(rows_half, d ^ 2)], axis=1
-            ).astype(bf16)
-            back = swap(away, "tensor", first).astype(f32)
-            onward = (block(rows_half, d ^ second) + back[:, out_cols:]).astype(bf16)
-            last = swap(onward, "tensor", second).astype(f32)
-            done.append(block(rows_half, d) + back[:, :out_cols] + last)
-        sums.append(jnp.stack(done).reshape(4, size, out_cols))
+    starts = [sum(CHUNKS[:k]) * hidden.shape[0] // 256 for k in range(len(CHUNKS) + 1)]
+    n = len(CHUNKS)
+    gathered, turned, sums, partials = [None] * n, [None] * n, [None] * n, [None] * n
+    order = table
+    for k in range(n + LAG):
+        if k < n:
+            a = hidden[starts[k] : starts[k + 1]]
+            if k >= AHEAD:
+                a = after(a, turned[k - AHEAD])
+            near = lax.ppermute(a, "tensor", inward)
+            far = lax.ppermute(a, "tensor", across)
+            last = lax.ppermute(near, "tensor", across)
+            own, other = turn(signs, table, a, near, far, last, order)
+            order = turned[k] = own
+            rot = jnp.where(inner, own, lax.ppermute(other, "tensor", outward))
+            x1 = swap(rot, "dp", 2)
+            gathered[k] = [rot, swap(rot, "dp", 1), x1, swap(x1, "dp", 1)]
+        j = k - LAG
+        if j >= 0:
+            partial = down(gathered[j], down_weight, order)
+            order = partial
+            away = jnp.concatenate([block(partial, d ^ 1), block(partial, d ^ 3)], axis=1)
+            back = swap(away.astype(bf16), "tensor", 1).astype(f32)
+            onward = (block(partial, d ^ 2) + back[:, out_cols:]).astype(bf16)
+            final = swap(onward, "tensor", 2).astype(f32)
+            done = block(partial, d) + back[:, :out_cols] + final
+            sums[j] = done.reshape(4, done.shape[0] // 4, out_cols)
     by_offset = jnp.concatenate(sums, axis=1)
     s0, s1, s2, s3 = by_offset
     low = rank & 1 == 1
@@ -138,10 +188,10 @@
     fits = (
         lax.axis_size("tensor") == 4
         and lax.axis_size("dp") == 4
-        and hidden.shape[0] % (16 * CHUNKS) == 0
+        and hidden.shape[0] % 256 == 0
         and hidden.shape[1] % WIDE == 0
     )
-    return (ring_of_four if fits else any_size)(hidden, down_weight, scales, residual)
+    return (line_of_four if fits else any_size)(hidden, down_weight, scales, residual)
 
 
 def solution(mesh):

time: 676 us -> 614 us (0.908)
  Pallas kernels: 27.3 us -> 244 us
  waiting for transfers between devices: 326 us -> 166 us
  matrix products: 100 us -> 0 us
  starting transfers between devices: 188 us -> 158 us
  local copies, waits for them, and re-layouts: 16.3 us -> 23.2 us
    ppermute x36 -> x45, waiting for transfers between devices: 326 us -> 85.1 us  [swap(): lax.ppermute(x, axis, [(i, i ^ mask) for i in range(lax.axis_size(axis))])]
    pallas_call x4 -> x18, Pallas kernels: 27.3 us -> 244 us  [the longest x9 200 us: down(): pl.pallas_call(down_kernel, grid=(units // step,), in_specs=[part] * 4 +...]
    ppermute x36 -> x45, starting transfers between devices: 188 us -> 51.6 us  [swap(): lax.ppermute(x, axis, [(i, i ^ mask) for i in range(lax.axis_size(axis))])]
    ppermute x0 -> x36, starting transfers between devices: none -> 106 us  [the longest x9 69.1 us: line_of_four(): near = lax.ppermute(a, 'tensor', inward)]
    dot_general x4 -> x0, matrix products: 100 us -> none  [ring_of_four(): partial = jnp.dot(tokens, down_weight, preferred_element_type=f32)]
    ppermute x0 -> x36, waiting for transfers between devices: none -> 81.2 us  [the longest x9 71.9 us: line_of_four(): near = lax.ppermute(a, 'tensor', inward)]
    unnamed x20 -> x70, local copies, waits for them, and re-layouts: 3.01 us -> 14.7 us
  transfers between devices with their start and end apart: 36 -> 81, of which waited for: 22 -> 21; matrix products, arithmetic and copies ran while one was open for 17% -> 4% of each run, Pallas kernels for 4% -> 40%
where the time goes in v1:
time: 614 us; the launch traced here: 611 us
  Pallas kernels  244 us (40%)
  waiting for transfers between devices  166 us (27%)
  starting transfers between devices  158 us (26%)
  local copies, waits for them, and re-layouts  23.2 us (4%)
  other arithmetic  19 us (3%)
    pallas_call x9, Pallas kernels, down(): pl.pallas_call(down_kernel, grid=(units // step,), in_specs=[part] * 4 +...  200 us
    ppermute x45, waiting for transfers between devices, swap(): lax.ppermute(x, axis, [(i, i ^ mask) for i in range(lax.axis_size(axis))])  85.1 us
    ppermute x9, waiting for transfers between devices, line_of_four(): near = lax.ppermute(a, 'tensor', inward)  71.9 us
    ppermute x9, starting transfers between devices, line_of_four(): near = lax.ppermute(a, 'tensor', inward)  69.1 us
    ppermute x45, starting transfers between devices, swap(): lax.ppermute(x, axis, [(i, i ^ mask) for i in range(lax.axis_size(axis))])  51.6 us
    pallas_call x9, Pallas kernels, turn(): pl.pallas_call(turn_kernel, grid=(units // step,), in_specs=[pl.BlockSpec...  44.1 us
    unnamed x70, local copies, waits for them, and re-layouts  14.7 us
    ppermute x9, starting transfers between devices, line_of_four(): last = lax.ppermute(near, 'tensor', across)  13.1 us
  transfers between devices with their start and end apart: 81, of which 21 were waited for; matrix products, arithmetic and copies ran while one was open for 4% of the time, Pallas kernels for 40%

profile of v1, /device:TPU:0, one launch (start us, length us, event | category | flops | bytes accessed | tf_op | source)
XLA Modules:
  0.0 611.0 jit_solution(5963465682841259140)
XLA Ops:
  0.0 4.5 fusion.25
  4.5 5.8 collective-permute-start
  10.4 2.3 collective-permute-start.10
  14.2 14.6 %collective-permute-done.near_ref = bf16[32,13312]{1,0:T(8,128)(2,1)} collective-permute-done((bf16[32,13312]{1,0:T(8,128)(2,1)S(1)}, bf16[32,13312]{1,0:T(8,128)(2,1)}, u32[]{:S(2)}, u32[]{:S(2)}) %collective-permute-start) | collective-permute-done | bytes 852000 | tf_op jit(solution)/shard_map/ppermute | solution.py:155
  32.2 13.7 %collective-permute-done.10.near_ref = bf16[32,13312]{1,0:T(8,128)(2,1)} collective-permute-done((bf16[32,13312]{1,0:T(8,128)(2,1)S(1)}, bf16[32,13312]{1,0:T(8,128)(2,1)}, u32[]{:S(2)}, u32[]{:S(2)}) %collective-permute-start.10) | collective-permute-done | bytes 852000 | tf_op jit(solution)/shard_map/ppermute | solution.py:155
  48.9 5.0 shard_map.46
  55.3 5.1 shard_map.47
  60.3 36.5 %collective-permute-start.19 = (bf16[32,13312]{1,0:T(8,128)(2,1)}, bf16[32,13312]{1,0:T(8,128)(2,1)}, u32[]{:S(2)}, u32[]{:S(2)}) collective-permute-start(bf16[32,13312]{1,0:T(8,128)(2,1)} %get-tuple-element.36.a_ref), channel_id=1, source_target_pairs={{0,4},{12,8},{1,5},{13,9},{2,6},{14,10},{3,7},{15,11},{16,20},{28,... | collective-permute-start | bytes 2555912 | tf_op jit(solution)/shard_map/ppermute | solution.py:155
  98.4 2.3 collective-permute-start.7
  104.0 25.6 %collective-permute-done.7.near_ref = bf16[32,13312]{1,0:T(8,128)(2,1)S(1)} collective-permute-done((bf16[32,13312]{1,0:T(8,128)(2,1)S(1)}, bf16[32,13312]{1,0:T(8,128)(2,1)S(1)}, u32[]{:S(2)}, u32[]{:S(2)}) %collective-permute-start.7) | collective-permute-done | bytes 852000 | tf_op jit(solution)/shard_map/ppermute | solution.py:155
  134.2 17.4 %collective-permute-done.5.t2 = bf16[32,13312]{1,0:T(8,128)(2,1)} collective-permute-done((bf16[32,13312]{1,0:T(8,128)(2,1)S(1)}, bf16[32,13312]{1,0:T(8,128)(2,1)}, u32[]{:S(2)}, u32[]{:S(2)}) %collective-permute-start.5) | collective-permute-done | bytes 852000 | tf_op jit(solution)/shard_map/ppermute | solution.py:18
  151.6 2.1 fusion.24
  154.2 10.4 %collective-permute-done.17.t2 = bf16[32,13312]{1,0:T(8,128)(2,1)S(1)} collective-permute-done((bf16[32,13312]{1,0:T(8,128)(2,1)S(1)}, bf16[32,13312]{1,0:T(8,128)(2,1)S(1)}, u32[]{:S(2)}, u32[]{:S(2)}) %collective-permute-start.17) | collective-permute-done | bytes 852000 | tf_op jit(solution)/shard_map/ppermute | solution.py:18
  166.0 5.0 shard_map.48
  171.1 5.4 collective-permute-start.28
  177.6 22.2 %shard_map.49.order_ref = f32[128,2048]{1,0:T(8,128)S(1)} custom-call(bf16[32,13312]{1,0:T(8,128)(2,1)S(1)} %broadcast_select_fusion.6.t0, bf16[32,13312]{1,0:T(8,128)(2,1)} %collective-permute-done.4.t1, bf16[32,13312]{1,0:T(8,128)(2,1)} %collective-permute-done.5.t2, bf16[32,13312]{1,0:T(8,128)(2,1)} %collective-permute-done.6.t3, ...), custom_call_target="tpu_custom_call" | custom-call | flops 6979321856 | bytes 54525952 | tf_op jit(solution)/shard_map/pallas_call | solution.py:110
  203.6 5.0 shard_map.50
  209.8 22.1 %shard_map.51.order_ref = f32[128,2048]{1,0:T(8,128)S(1)} custom-call(bf16[32,13312]{1,0:T(8,128)(2,1)S(1)} %broadcast_select_fusion.5.t0, bf16[32,13312]{1,0:T(8,128)(2,1)} %collective-permute-done.16.t1, bf16[32,13312]{1,0:T(8,128)(2,1)S(1)} %collective-permute-done.17.t2, bf16[32,13312]{1,0:T(8,128)(2,1)} %collective-permute-done.18.t3, ...), custom_call_target="tpu_custom_call" | custom-call | flops 6979321856 | bytes 54525952 | tf_op jit(solution)/shard_map/pallas_call | solution.py:110
  232.0 3.6 collective-permute-start.22
  238.6 9.0 %collective-permute-done.13 = bf16[128,1024]{1,0:T(8,128)(2,1)S(1)} collective-permute-done((bf16[128,1024]{1,0:T(8,128)(2,1)S(1)}, bf16[128,1024]{1,0:T(8,128)(2,1)S(1)}, u32[]{:S(2)}, u32[]{:S(2)}) %collective-permute-start.13) | collective-permute-done | bytes 262176 | tf_op jit(solution)/shard_map/ppermute | solution.py:18
  249.0 3.8 collective-permute-start.14
  252.9 5.6 collective-permute-done.14
  259.4 6.0 collective-permute-done.23
  266.2 2.2 collective-permute-start.37
  270.0 5.4 collective-permute-done.33
  275.4 1.6 collective-permute-start.38
  278.6 5.0 shard_map.52
  283.9 3.0 collective-permute-done.37.near_ref
  288.2 1.7 collective-permute-start.39
  292.2 22.0 %shard_map.53.order_ref = f32[128,2048]{1,0:T(8,128)S(1)} custom-call(bf16[32,13312]{1,0:T(8,128)(2,1)S(1)} %broadcast_select_fusion.4.t0, bf16[32,13312]{1,0:T(8,128)(2,1)} %collective-permute-done.25.t1, bf16[32,13312]{1,0:T(8,128)(2,1)S(1)} %copy-done.18, bf16[32,13312]{1,0:T(8,128)(2,1)} %collective-permute-done.27.t3, bf16[13312,2048]{1,0:T(8,128)(2,1)} %weight_ref.17, ...), custom_call_target="tpu_custom_call" | custom-call | flops 6979321856 | bytes 54525952 | tf_op jit(solution)/shard_map/pallas_call | solution.py:110
  314.3 11.5 %collective-permute-start.31 = (bf16[128,1024]{1,0:T(8,128)(2,1)S(1)}, bf16[128,1024]{1,0:T(8,128)(2,1)S(1)}, u32[]{:S(2)}, u32[]{:S(2)}) collective-permute-start(bf16[128,1024]{1,0:T(8,128)(2,1)S(1)} %pad_maximum_fusion.2), channel_id=1, source_target_pairs={{0,4},{4,0},{8,12},{12,8},{1,5},{5,1},{9,13},{13,9},{2,6},{6,2},{1... | collective-permute-start | bytes 786440 | tf_op jit(solution)/shard_map/ppermute | solution.py:18
  326.9 3.2 collective-permute-start.46
  331.6 5.0 shard_map.54
  339.8 3.3 collective-permute-start.32
  344.3 22.2 %shard_map.55.order_ref = f32[128,2048]{1,0:T(8,128)S(1)} custom-call(bf16[32,13312]{1,0:T(8,128)(2,1)S(1)} %copy-done.8, bf16[32,13312]{1,0:T(8,128)(2,1)} %collective-permute-done.34.t1, bf16[32,13312]{1,0:T(8,128)(2,1)} %collective-permute-done.35.t2, bf16[32,13312]{1,0:T(8,128)(2,1)} %collective-permute-done.36.t3, bf16[13312,2048]{1,0:T(8,128)(2,1)} %weight_ref.17, ...), custom_call_target="tpu_custom_call" | custom-call | flops 6979321856 | bytes 54525952 | tf_op jit(solution)/shard_map/pallas_call | solution.py:110
  368.6 5.5 collective-permute-done.40
  374.2 3.0 collective-permute-start.55
  377.1 1.6 collective-permute-start.48
  379.6 7.2 %collective-permute-done.55.near_ref = bf16[16,13312]{1,0:T(8,128)(2,1)} collective-permute-done((bf16[16,13312]{1,0:T(8,128)(2,1)}, bf16[16,13312]{1,0:T(8,128)(2,1)}, u32[]{:S(2)}, u32[]{:S(2)}) %collective-permute-start.55) | collective-permute-done | bytes 426016 | tf_op jit(solution)/shard_map/ppermute | solution.py:155
  388.9 5.0 shard_map.56
  393.9 10.8 %collective-permute-done.41 = bf16[128,512]{1,0:T(8,128)(2,1)S(1)} collective-permute-done((bf16[128,512]{1,0:T(8,128)(2,1)S(1)}, bf16[128,512]{1,0:T(8,128)(2,1)S(1)}, u32[]{:S(2)}, u32[]{:S(2)}) %collective-permute-start.41) | collective-permute-done | bytes 131104 | tf_op jit(solution)/shard_map/ppermute | solution.py:18
  410.3 22.3 %shard_map.57.order_ref = f32[128,2048]{1,0:T(8,128)S(1)} custom-call(bf16[32,13312]{1,0:T(8,128)(2,1)} %broadcast_select_fusion.2.t0, bf16[32,13312]{1,0:T(8,128)(2,1)} %collective-permute-done.43.t1, bf16[32,13312]{1,0:T(8,128)(2,1)} %collective-permute-done.44.t2, bf16[32,13312]{1,0:T(8,128)(2,1)} %collective-permute-done.45.t3, ...), custom_call_target="tpu_custom_call" | custom-call | flops 6979321856 | bytes 54525952 | tf_op jit(solution)/shard_map/pallas_call | solution.py:110
  432.8 8.5 %collective-permute-start.64 = (bf16[16,13312]{1,0:T(8,128)(2,1)}, bf16[16,13312]{1,0:T(8,128)(2,1)}, u32[]{:S(2)}, u32[]{:S(2)}) collective-permute-start(bf16[16,13312]{1,0:T(8,128)(2,1)} %get-tuple-element.51.a_ref), channel_id=1, source_target_pairs={{0,4},{12,8},{1,5},{13,9},{2,6},{14,10},{3,7},{15,11},{16,20},{28,... | collective-permute-start | bytes 1277960 | tf_op jit(solution)/shard_map/ppermute | solution.py:155
  443.1 7.8 %collective-permute-done.64.near_ref = bf16[16,13312]{1,0:T(8,128)(2,1)} collective-permute-done((bf16[16,13312]{1,0:T(8,128)(2,1)}, bf16[16,13312]{1,0:T(8,128)(2,1)}, u32[]{:S(2)}, u32[]{:S(2)}) %collective-permute-start.64) | collective-permute-done | bytes 426016 | tf_op jit(solution)/shard_map/ppermute | solution.py:155
  452.3 4.5 shard_map.58
  457.5 1.6 fusion.6
  461.4 22.2 %shard_map.59.order_ref = f32[128,2048]{1,0:T(8,128)S(1)} custom-call(bf16[32,13312]{1,0:T(8,128)(2,1)S(1)} %broadcast_select_fusion.1.t0, bf16[32,13312]{1,0:T(8,128)(2,1)} %collective-permute-done.52.t1, bf16[32,13312]{1,0:T(8,128)(2,1)} %collective-permute-done.53.t2, bf16[32,13312]{1,0:T(8,128)(2,1)} %collective-permute-done.54.t3, ...), custom_call_target="tpu_custom_call" | custom-call | flops 6979321856 | bytes 54525952 | tf_op jit(solution)/shard_map/pallas_call | solution.py:110
  484.6 4.1 collective-permute-start.58
  490.7 4.5 shard_map.60
  495.2 3.5 collective-permute-done.58
  501.0 3.1 collective-permute-start.59
  506.4 4.0 collective-permute-done.59
  511.4 3.8 collective-permute-done.75
  516.9 22.0 %shard_map.61.order_ref = f32[128,2048]{1,0:T(8,128)S(1)} custom-call(bf16[32,13312]{1,0:T(8,128)(2,1)S(1)} %broadcast_select_fusion.t0, bf16[32,13312]{1,0:T(8,128)(2,1)} %collective-permute-done.61.t1, bf16[32,13312]{1,0:T(8,128)(2,1)} %collective-permute-done.62.t2, bf16[32,13312]{1,0:T(8,128)(2,1)S(1)} %collective-permute-done.63.t3, ...), custom_call_target="tpu_custom_call" | custom-call | flops 6979321856 | bytes 54525952 | tf_op jit(solution)/shard_map/pallas_call | solution.py:110
  538.9 22.3 %shard_map.62.order_ref = f32[64,2048]{1,0:T(8,128)S(1)} custom-call(bf16[16,13312]{1,0:T(8,128)(2,1)S(1)} %broadcast_select_fusion.8.t0, bf16[16,13312]{1,0:T(8,128)(2,1)S(1)} %collective-permute-done.70.t1, bf16[16,13312]{1,0:T(8,128)(2,1)S(1)} %collective-permute-done.71.t2, bf16[16,13312]{1,0:T(8,128)(2,1)S(1)} %collective-permute-done.72.t3, ...), custom_call_target="tpu_custom_call" | custom-call | flops 3489660928 | bytes 54525952 | tf_op jit(solution)/shard_map/pallas_call | solution.py:110
  561.4 2.1 collective-permute-start.67
  563.5 5.0 collective-permute-done.73
  569.8 3.9 collective-permute-done.74
  574.2 22.3 %shard_map.63 = f32[64,2048]{1,0:T(8,128)S(1)} custom-call(bf16[16,13312]{1,0:T(8,128)(2,1)S(1)} %broadcast_select_fusion.7.t0, bf16[16,13312]{1,0:T(8,128)(2,1)S(1)} %collective-permute-done.76.t1, bf16[16,13312]{1,0:T(8,128)(2,1)S(1)} %collective-permute-done.77.t2, bf16[16,13312]{1,0:T(8,128)(2,1)S(1)} %collective-permute-done.78.t3, ...), custom_call_target="tpu_custom_call" | custom-call | flops 3489660928 | bytes 54525952 | tf_op jit(solution)/shard_map/pallas_call | solution.py:110
  596.6 2.3 collective-permute-start.79
  599.6 2.1 collective-permute-done.79
  601.8 2.8 collective-permute-start.80
  605.3 1.7 collective-permute-done.80
  607.7 1.9 select_bitcast_fusion.3
  (252 shorter events, 79.3 us)
Async XLA Ops:
  4.5 24.3 %collective-permute-start = (bf16[32,13312]{1,0:T(8,128)(2,1)S(1)}, bf16[32,13312]{1,0:T(8,128)(2,1)}, u32[]{:S(2)}, u32[]{:S(2)}) collective-permute-start(bf16[32,13312]{1,0:T(8,128)(2,1)S(1)} %get-tuple-element.63.a_ref), channel_id=1, source_target_pairs={{0,4},{12,8},{1,5},{13,9},{2,6},{14,10},{3,7},{15,11},{16,20},{28,... | collective-permute-start | bytes 2555912 | tf_op jit(solution)/shard_map/ppermute | solution.py:155
  10.4 35.5 %collective-permute-start.10 = (bf16[32,13312]{1,0:T(8,128)(2,1)S(1)}, bf16[32,13312]{1,0:T(8,128)(2,1)}, u32[]{:S(2)}, u32[]{:S(2)}) collective-permute-start(bf16[32,13312]{1,0:T(8,128)(2,1)S(1)} %get-tuple-element.61.a_ref), channel_id=1, source_target_pairs={{0,4},{12,8},{1,5},{13,9},{2,6},{14,10},{3,7},{15,11},{16,20},{28,... | collective-permute-start | bytes 2555912 | tf_op jit(solution)/shard_map/ppermute | solution.py:155
  12.6 36.3 %collective-permute-start.1 = (bf16[32,13312]{1,0:T(8,128)(2,1)S(1)}, bf16[32,13312]{1,0:T(8,128)(2,1)}, u32[]{:S(2)}, u32[]{:S(2)}) collective-permute-start(bf16[32,13312]{1,0:T(8,128)(2,1)S(1)} %get-tuple-element.63.a_ref), channel_id=1, source_target_pairs={{4,8},{8,4},{5,9},{9,5},{6,10},{10,6},{7,11},{11,7},{20,24},{24,20... | collective-permute-start | bytes 2555912 | tf_op jit(solution)/shard_map/ppermute | solution.py:156
  28.8 20.1 %collective-permute-start.2 = (bf16[32,13312]{1,0:T(8,128)(2,1)}, bf16[32,13312]{1,0:T(8,128)(2,1)}, u32[]{:S(2)}, u32[]{:S(2)}) collective-permute-start(bf16[32,13312]{1,0:T(8,128)(2,1)} %collective-permute-done.near_ref), channel_id=1, source_target_pairs={{4,8},{8,4},{5,9},{9,5},{6,10},{10,6},{7,11},{11,7},{20,24},{24,20... | collective-permute-start | bytes 2555912 | tf_op jit(solution)/shard_map/ppermute | solution.py:157
  30.4 24.9 %collective-permute-start.11 = (bf16[32,13312]{1,0:T(8,128)(2,1)S(1)}, bf16[32,13312]{1,0:T(8,128)(2,1)}, u32[]{:S(2)}, u32[]{:S(2)}) collective-permute-start(bf16[32,13312]{1,0:T(8,128)(2,1)S(1)} %get-tuple-element.61.a_ref), channel_id=1, source_target_pairs={{4,8},{8,4},{5,9},{9,5},{6,10},{10,6},{7,11},{11,7},{20,24},{24,20... | collective-permute-start | bytes 2555912 | tf_op jit(solution)/shard_map/ppermute | solution.py:156
  53.9 47.5 %collective-permute-start.3 = (bf16[32,13312]{1,0:T(8,128)(2,1)}, bf16[32,13312]{1,0:T(8,128)(2,1)}, u32[]{:S(2)}, u32[]{:S(2)}) collective-permute-start(bf16[32,13312]{1,0:T(8,128)(2,1)} %get-tuple-element.31), channel_id=1, source_target_pairs={{4,0},{8,12},{5,1},{9,13},{6,2},{10,14},{7,3},{11,15},{20,16},{24,... | collective-permute-start | bytes 2555912 | tf_op jit(solution)/shard_map/ppermute | solution.py:160
  60.3 71.6 %collective-permute-start.19 = (bf16[32,13312]{1,0:T(8,128)(2,1)}, bf16[32,13312]{1,0:T(8,128)(2,1)}, u32[]{:S(2)}, u32[]{:S(2)}) collective-permute-start(bf16[32,13312]{1,0:T(8,128)(2,1)} %get-tuple-element.36.a_ref), channel_id=1, source_target_pairs={{0,4},{12,8},{1,5},{13,9},{2,6},{14,10},{3,7},{15,11},{16,20},{28,... | collective-permute-start | bytes 2555912 | tf_op jit(solution)/shard_map/ppermute | solution.py:155
  96.9 103.9 %collective-permute-start.20 = (bf16[32,13312]{1,0:T(8,128)(2,1)}, bf16[32,13312]{1,0:T(8,128)(2,1)}, u32[]{:S(2)}, u32[]{:S(2)}) collective-permute-start(bf16[32,13312]{1,0:T(8,128)(2,1)} %get-tuple-element.36.a_ref), channel_id=1, source_target_pairs={{4,8},{8,4},{5,9},{9,5},{6,10},{10,6},{7,11},{11,7},{20,24},{24,20... | collective-permute-start | bytes 2555912 | tf_op jit(solution)/shard_map/ppermute | solution.py:156
  98.4 31.2 %collective-permute-start.7 = (bf16[32,13312]{1,0:T(8,128)(2,1)S(1)}, bf16[32,13312]{1,0:T(8,128)(2,1)S(1)}, u32[]{:S(2)}, u32[]{:S(2)}) collective-permute-start(bf16[32,13312]{1,0:T(8,128)(2,1)S(1)} %get-tuple-element.32.a_ref), channel_id=1, source_target_pairs={{0,4},{12,8},{1,5},{13,9},{2,6},{14,10},{3,7},{15,11},{16,20},{28,... | collective-permute-start | bytes 2555912 | tf_op jit(solution)/shard_map/ppermute | solution.py:155
  100.7 31.3 %collective-permute-start.8 = (bf16[32,13312]{1,0:T(8,128)(2,1)S(1)}, bf16[32,13312]{1,0:T(8,128)(2,1)S(1)}, u32[]{:S(2)}, u32[]{:S(2)}) collective-permute-start(bf16[32,13312]{1,0:T(8,128)(2,1)S(1)} %get-tuple-element.32.a_ref), channel_id=1, source_target_pairs={{4,8},{8,4},{5,9},{9,5},{6,10},{10,6},{7,11},{11,7},{20,24},{24,20... | collective-permute-start | bytes 2555912 | tf_op jit(solution)/shard_map/ppermute | solution.py:156
  101.5 29.6 %collective-permute-start.15 = (bf16[32,13312]{1,0:T(8,128)(2,1)}, bf16[32,13312]{1,0:T(8,128)(2,1)S(1)}, u32[]{:S(2)}, u32[]{:S(2)}) collective-permute-start(bf16[32,13312]{1,0:T(8,128)(2,1)} %get-tuple-element.35), channel_id=1, source_target_pairs={{4,0},{8,12},{5,1},{9,13},{6,2},{10,14},{7,3},{11,15},{20,16},{24,... | collective-permute-start | bytes 2555912 | tf_op jit(solution)/shard_map/ppermute | solution.py:160
  129.6 22.0 %collective-permute-start.5 = (bf16[32,13312]{1,0:T(8,128)(2,1)S(1)}, bf16[32,13312]{1,0:T(8,128)(2,1)}, u32[]{:S(2)}, u32[]{:S(2)}) collective-permute-start(bf16[32,13312]{1,0:T(8,128)(2,1)S(1)} %broadcast_select_fusion.6.t0), channel_id=1, source_target_pairs={{0,2},{1,3},{2,0},{3,1},{4,6},{5,7},{6,4},{7,5},{8,10},{9,11},{10,... | collective-permute-start | bytes 2555912 | tf_op jit(solution)/shard_map/ppermute | solution.py:18
  131.9 21.8 %collective-permute-start.4 = (bf16[32,13312]{1,0:T(8,128)(2,1)S(1)}, bf16[32,13312]{1,0:T(8,128)(2,1)}, u32[]{:S(2)}, u32[]{:S(2)}) collective-permute-start(bf16[32,13312]{1,0:T(8,128)(2,1)S(1)} %broadcast_select_fusion.6.t0), channel_id=1, source_target_pairs={{0,1},{1,0},{2,3},{3,2},{4,5},{5,4},{6,7},{7,6},{8,9},{9,8},{10,11... | collective-permute-start | bytes 2555912 | tf_op jit(solution)/shard_map/ppermute | solution.py:18
  132.0 32.6 %collective-permute-start.17 = (bf16[32,13312]{1,0:T(8,128)(2,1)S(1)}, bf16[32,13312]{1,0:T(8,128)(2,1)S(1)}, u32[]{:S(2)}, u32[]{:S(2)}) collective-permute-start(bf16[32,13312]{1,0:T(8,128)(2,1)S(1)} %broadcast_select_fusion.5.t0), channel_id=1, source_target_pairs={{0,2},{1,3},{2,0},{3,1},{4,6},{5,7},{6,4},{7,5},{8,10},{9,11},{10,... | collective-permute-start | bytes 2555912 | tf_op jit(solution)/shard_map/ppermute | solution.py:18
  132.6 69.7 %collective-permute-start.21 = (bf16[32,13312]{1,0:T(8,128)(2,1)}, bf16[32,13312]{1,0:T(8,128)(2,1)}, u32[]{:S(2)}, u32[]{:S(2)}) collective-permute-start(bf16[32,13312]{1,0:T(8,128)(2,1)} %collective-permute-done.19.near_ref), channel_id=1, source_target_pairs={{4,8},{8,4},{5,9},{9,5},{6,10},{10,6},{7,11},{11,7},{20,24},{24,20... | collective-permute-start | bytes 2555912 | tf_op jit(solution)/shard_map/ppermute | solution.py:157
  151.6 19.5 %collective-permute-start.6 = (bf16[32,13312]{1,0:T(8,128)(2,1)}, bf16[32,13312]{1,0:T(8,128)(2,1)}, u32[]{:S(2)}, u32[]{:S(2)}) collective-permute-start(bf16[32,13312]{1,0:T(8,128)(2,1)} %collective-permute-done.5.t2), channel_id=1, source_target_pairs={{0,1},{1,0},{2,3},{3,2},{4,5},{5,4},{6,7},{7,6},{8,9},{9,8},{10,11... | collective-permute-start | bytes 2555912 | tf_op jit(solution)/shard_map/ppermute | solution.py:18
  153.7 54.9 %collective-permute-start.16 = (bf16[32,13312]{1,0:T(8,128)(2,1)S(1)}, bf16[32,13312]{1,0:T(8,128)(2,1)}, u32[]{:S(2)}, u32[]{:S(2)}) collective-permute-start(bf16[32,13312]{1,0:T(8,128)(2,1)S(1)} %broadcast_select_fusion.5.t0), channel_id=1, source_target_pairs={{0,1},{1,0},{2,3},{3,2},{4,5},{5,4},{6,7},{7,6},{8,9},{9,8},{10,11... | collective-permute-start | bytes 2555912 | tf_op jit(solution)/shard_map/ppermute | solution.py:18
  164.7 44.0 %collective-permute-start.18 = (bf16[32,13312]{1,0:T(8,128)(2,1)S(1)}, bf16[32,13312]{1,0:T(8,128)(2,1)}, u32[]{:S(2)}, u32[]{:S(2)}) collective-permute-start(bf16[32,13312]{1,0:T(8,128)(2,1)S(1)} %collective-permute-done.17.t2), channel_id=1, source_target_pairs={{0,1},{1,0},{2,3},{3,2},{4,5},{5,4},{6,7},{7,6},{8,9},{9,8},{10,11... | collective-permute-start | bytes 2555912 | tf_op jit(solution)/shard_map/ppermute | solution.py:18
  171.1 95.1 %collective-permute-start.28 = (bf16[32,13312]{1,0:T(8,128)(2,1)}, bf16[32,13312]{1,0:T(8,128)(2,1)}, u32[]{:S(2)}, u32[]{:S(2)}) collective-permute-start(bf16[32,13312]{1,0:T(8,128)(2,1)} %get-tuple-element.39.a_ref), channel_id=1, source_target_pairs={{0,4},{12,8},{1,5},{13,9},{2,6},{14,10},{3,7},{15,11},{16,20},{28,... | collective-permute-start | bytes 2555912 | tf_op jit(solution)/shard_map/ppermute | solution.py:155
  200.8 74.6 %collective-permute-start.29 = (bf16[32,13312]{1,0:T(8,128)(2,1)}, bf16[32,13312]{1,0:T(8,128)(2,1)}, u32[]{:S(2)}, u32[]{:S(2)}) collective-permute-start(bf16[32,13312]{1,0:T(8,128)(2,1)} %get-tuple-element.39.a_ref), channel_id=1, source_target_pairs={{4,8},{8,4},{5,9},{9,5},{6,10},{10,6},{7,11},{11,7},{20,24},{24,20... | collective-permute-start | bytes 2555912 | tf_op jit(solution)/shard_map/ppermute | solution.py:156
  202.4 33.4 %collective-permute-start.24 = (bf16[32,13312]{1,0:T(8,128)(2,1)}, bf16[32,13312]{1,0:T(8,128)(2,1)}, u32[]{:S(2)}, u32[]{:S(2)}) collective-permute-start(bf16[32,13312]{1,0:T(8,128)(2,1)} %get-tuple-element.38), channel_id=1, source_target_pairs={{4,0},{8,12},{5,1},{9,13},{6,2},{10,14},{7,3},{11,15},{20,16},{24,... | collective-permute-start | bytes 2555912 | tf_op jit(solution)/shard_map/ppermute | solution.py:160
  232.0 17.0 %collective-permute-start.22 = (bf16[128,1024]{1,0:T(8,128)(2,1)S(1)}, bf16[128,1024]{1,0:T(8,128)(2,1)S(1)}, u32[]{:S(2)}, u32[]{:S(2)}) collective-permute-start(bf16[128,1024]{1,0:T(8,128)(2,1)S(1)} %pad_maximum_fusion.1), channel_id=1, source_target_pairs={{0,4},{4,0},{8,12},{12,8},{1,5},{5,1},{9,13},{13,9},{2,6},{6,2},{1... | collective-permute-start | bytes 786440 | tf_op jit(solution)/shard_map/ppermute | solution.py:18
  237.0 31.4 %collective-permute-start.26 = (bf16[32,13312]{1,0:T(8,128)(2,1)S(1)}, bf16[32,13312]{1,0:T(8,128)(2,1)S(1)}, u32[]{:S(2)}, u32[]{:S(2)}) collective-permute-start(bf16[32,13312]{1,0:T(8,128)(2,1)S(1)} %broadcast_select_fusion.4.t0), channel_id=1, source_target_pairs={{0,2},{1,3},{2,0},{3,1},{4,6},{5,7},{6,4},{7,5},{8,10},{9,11},{10,... | collective-permute-start | bytes 2555912 | tf_op jit(solution)/shard_map/ppermute | solution.py:18
  247.6 27.7 %collective-permute-start.33 = (bf16[32,13312]{1,0:T(8,128)(2,1)S(1)}, bf16[32,13312]{1,0:T(8,128)(2,1)S(1)}, u32[]{:S(2)}, u32[]{:S(2)}) collective-permute-start(bf16[32,13312]{1,0:T(8,128)(2,1)S(1)} %copy-done.30), channel_id=1, source_target_pairs={{4,0},{8,12},{5,1},{9,13},{6,2},{10,14},{7,3},{11,15},{20,16},{24,... | collective-permute-start | bytes 2555912 | tf_op jit(solution)/shard_map/ppermute | solution.py:160
  265.4 18.2 %collective-permute-start.25 = (bf16[32,13312]{1,0:T(8,128)(2,1)S(1)}, bf16[32,13312]{1,0:T(8,128)(2,1)}, u32[]{:S(2)}, u32[]{:S(2)}) collective-permute-start(bf16[32,13312]{1,0:T(8,128)(2,1)S(1)} %broadcast_select_fusion.4.t0), channel_id=1, source_target_pairs={{0,1},{1,0},{2,3},{3,2},{4,5},{5,4},{6,7},{7,6},{8,9},{9,8},{10,11... | collective-permute-start | bytes 2555912 | tf_op jit(solution)/shard_map/ppermute | solution.py:18
  266.2 20.7 %collective-permute-start.37 = (bf16[32,13312]{1,0:T(8,128)(2,1)}, bf16[32,13312]{1,0:T(8,128)(2,1)}, u32[]{:S(2)}, u32[]{:S(2)}) collective-permute-start(bf16[32,13312]{1,0:T(8,128)(2,1)} %get-tuple-element.42.a_ref), channel_id=1, source_target_pairs={{0,4},{12,8},{1,5},{13,9},{2,6},{14,10},{3,7},{15,11},{16,20},{28,... | collective-permute-start | bytes 2555912 | tf_op jit(solution)/shard_map/ppermute | solution.py:155
  275.3 12.9 %collective-permute-start.27 = (bf16[32,13312]{1,0:T(8,128)(2,1)S(1)}, bf16[32,13312]{1,0:T(8,128)(2,1)}, u32[]{:S(2)}, u32[]{:S(2)}) collective-permute-start(bf16[32,13312]{1,0:T(8,128)(2,1)S(1)} %collective-permute-done.26.t2), channel_id=1, source_target_pairs={{0,1},{1,0},{2,3},{3,2},{4,5},{5,4},{6,7},{7,6},{8,9},{9,8},{10,11... | collective-permute-start | bytes 2555912 | tf_op jit(solution)/shard_map/ppermute | solution.py:18
  275.4 51.4 %collective-permute-start.38 = (bf16[32,13312]{1,0:T(8,128)(2,1)}, bf16[32,13312]{1,0:T(8,128)(2,1)}, u32[]{:S(2)}, u32[]{:S(2)}) collective-permute-start(bf16[32,13312]{1,0:T(8,128)(2,1)} %get-tuple-element.42.a_ref), channel_id=1, source_target_pairs={{4,8},{8,4},{5,9},{9,5},{6,10},{10,6},{7,11},{11,7},{20,24},{24,20... | collective-permute-start | bytes 2555912 | tf_op jit(solution)/shard_map/ppermute | solution.py:156
  277.1 37.2 %collective-permute-start.35 = (bf16[32,13312]{1,0:T(8,128)(2,1)S(1)}, bf16[32,13312]{1,0:T(8,128)(2,1)}, u32[]{:S(2)}, u32[]{:S(2)}) collective-permute-start(bf16[32,13312]{1,0:T(8,128)(2,1)S(1)} %broadcast_select_fusion.3.t0), channel_id=1, source_target_pairs={{0,2},{1,3},{2,0},{3,1},{4,6},{5,7},{6,4},{7,5},{8,10},{9,11},{10,... | collective-permute-start | bytes 2555912 | tf_op jit(solution)/shard_map/ppermute | solution.py:18
  283.7 54.7 %collective-permute-start.34 = (bf16[32,13312]{1,0:T(8,128)(2,1)S(1)}, bf16[32,13312]{1,0:T(8,128)(2,1)}, u32[]{:S(2)}, u32[]{:S(2)}) collective-permute-start(bf16[32,13312]{1,0:T(8,128)(2,1)S(1)} %broadcast_select_fusion.3.t0), channel_id=1, source_target_pairs={{0,1},{1,0},{2,3},{3,2},{4,5},{5,4},{6,7},{7,6},{8,9},{9,8},{10,11... | collective-permute-start | bytes 2555912 | tf_op jit(solution)/shard_map/ppermute | solution.py:18
  286.9 38.9 %collective-permute-start.42 = (bf16[32,13312]{1,0:T(8,128)(2,1)}, bf16[32,13312]{1,0:T(8,128)(2,1)S(1)}, u32[]{:S(2)}, u32[]{:S(2)}) collective-permute-start(bf16[32,13312]{1,0:T(8,128)(2,1)} %get-tuple-element.44), channel_id=1, source_target_pairs={{4,0},{8,12},{5,1},{9,13},{6,2},{10,14},{7,3},{11,15},{20,16},{24,... | collective-permute-start | bytes 2555912 | tf_op jit(solution)/shard_map/ppermute | solution.py:160
  288.2 41.8 %collective-permute-start.39 = (bf16[32,13312]{1,0:T(8,128)(2,1)}, bf16[32,13312]{1,0:T(8,128)(2,1)}, u32[]{:S(2)}, u32[]{:S(2)}) collective-permute-start(bf16[32,13312]{1,0:T(8,128)(2,1)} %collective-permute-done.37.near_ref), channel_id=1, source_target_pairs={{4,8},{8,4},{5,9},{9,5},{6,10},{10,6},{7,11},{11,7},{20,24},{24,20... | collective-permute-start | bytes 2555912 | tf_op jit(solution)/shard_map/ppermute | solution.py:157
  314.3 22.4 %collective-permute-start.31 = (bf16[128,1024]{1,0:T(8,128)(2,1)S(1)}, bf16[128,1024]{1,0:T(8,128)(2,1)S(1)}, u32[]{:S(2)}, u32[]{:S(2)}) collective-permute-start(bf16[128,1024]{1,0:T(8,128)(2,1)S(1)} %pad_maximum_fusion.2), channel_id=1, source_target_pairs={{0,4},{4,0},{8,12},{12,8},{1,5},{5,1},{9,13},{13,9},{2,6},{6,2},{1... | collective-permute-start | bytes 786440 | tf_op jit(solution)/shard_map/ppermute | solution.py:18
  325.8 14.0 %collective-permute-start.36 = (bf16[32,13312]{1,0:T(8,128)(2,1)}, bf16[32,13312]{1,0:T(8,128)(2,1)}, u32[]{:S(2)}, u32[]{:S(2)}) collective-permute-start(bf16[32,13312]{1,0:T(8,128)(2,1)} %collective-permute-done.35.t2), channel_id=1, source_target_pairs={{0,1},{1,0},{2,3},{3,2},{4,5},{5,4},{6,7},{7,6},{8,9},{9,8},{10,11... | collective-permute-start | bytes 2555912 | tf_op jit(solution)/shard_map/ppermute | solution.py:18
  326.9 47.3 %collective-permute-start.46 = (bf16[32,13312]{1,0:T(8,128)(2,1)}, bf16[32,13312]{1,0:T(8,128)(2,1)}, u32[]{:S(2)}, u32[]{:S(2)}) collective-permute-start(bf16[32,13312]{1,0:T(8,128)(2,1)} %get-tuple-element.45.a_ref), channel_id=1, source_target_pairs={{0,4},{12,8},{1,5},{13,9},{2,6},{14,10},{3,7},{15,11},{16,20},{28,... | collective-permute-start | bytes 2555912 | tf_op jit(solution)/shard_map/ppermute | solution.py:155
  330.1 47.1 %collective-permute-start.47 = (bf16[32,13312]{1,0:T(8,128)(2,1)}, bf16[32,13312]{1,0:T(8,128)(2,1)}, u32[]{:S(2)}, u32[]{:S(2)}) collective-permute-start(bf16[32,13312]{1,0:T(8,128)(2,1)} %get-tuple-element.45.a_ref), channel_id=1, source_target_pairs={{4,8},{8,4},{5,9},{9,5},{6,10},{10,6},{7,11},{11,7},{20,24},{24,20... | collective-permute-start | bytes 2555912 | tf_op jit(solution)/shard_map/ppermute | solution.py:156
  336.7 42.1 %collective-permute-start.44 = (bf16[32,13312]{1,0:T(8,128)(2,1)}, bf16[32,13312]{1,0:T(8,128)(2,1)}, u32[]{:S(2)}, u32[]{:S(2)}) collective-permute-start(bf16[32,13312]{1,0:T(8,128)(2,1)} %broadcast_select_fusion.2.t0), channel_id=1, source_target_pairs={{0,2},{1,3},{2,0},{3,1},{4,6},{5,7},{6,4},{7,5},{8,10},{9,11},{10,... | collective-permute-start | bytes 2555912 | tf_op jit(solution)/shard_map/ppermute | solution.py:18
  338.3 40.7 %collective-permute-start.51 = (bf16[32,13312]{1,0:T(8,128)(2,1)}, bf16[32,13312]{1,0:T(8,128)(2,1)S(1)}, u32[]{:S(2)}, u32[]{:S(2)}) collective-permute-start(bf16[32,13312]{1,0:T(8,128)(2,1)} %get-tuple-element.47), channel_id=1, source_target_pairs={{4,0},{8,12},{5,1},{9,13},{6,2},{10,14},{7,3},{11,15},{20,16},{24,... | collective-permute-start | bytes 2555912 | tf_op jit(solution)/shard_map/ppermute | solution.py:160
  339.8 26.8 %collective-permute-start.32 = (bf16[128,512]{1,0:T(8,128)(2,1)S(1)}, bf16[128,512]{1,0:T(8,128)(2,1)S(1)}, u32[]{:S(2)}, u32[]{:S(2)}) collective-permute-start(bf16[128,512]{1,0:T(8,128)(2,1)S(1)} %fusion.10), channel_id=1, source_target_pairs={{0,8},{4,12},{8,0},{12,4},{1,9},{5,13},{9,1},{13,5},{2,10},{6,14},... | collective-permute-start | bytes 393224 | tf_op jit(solution)/shard_map/ppermute | solution.py:18
  374.1 33.8 %collective-permute-start.43 = (bf16[32,13312]{1,0:T(8,128)(2,1)}, bf16[32,13312]{1,0:T(8,128)(2,1)}, u32[]{:S(2)}, u32[]{:S(2)}) collective-permute-start(bf16[32,13312]{1,0:T(8,128)(2,1)} %broadcast_select_fusion.2.t0), channel_id=1, source_target_pairs={{0,1},{1,0},{2,3},{3,2},{4,5},{5,4},{6,7},{7,6},{8,9},{9,8},{10,11... | collective-permute-start | bytes 2555912 | tf_op jit(solution)/shard_map/ppermute | solution.py:18
  374.2 12.6 %collective-permute-start.55 = (bf16[16,13312]{1,0:T(8,128)(2,1)}, bf16[16,13312]{1,0:T(8,128)(2,1)}, u32[]{:S(2)}, u32[]{:S(2)}) collective-permute-start(bf16[16,13312]{1,0:T(8,128)(2,1)} %get-tuple-element.48.a_ref), channel_id=1, source_target_pairs={{0,4},{12,8},{1,5},{13,9},{2,6},{14,10},{3,7},{15,11},{16,20},{28,... | collective-permute-start | bytes 1277960 | tf_op jit(solution)/shard_map/ppermute | solution.py:155
  378.8 29.1 %collective-permute-start.45 = (bf16[32,13312]{1,0:T(8,128)(2,1)}, bf16[32,13312]{1,0:T(8,128)(2,1)}, u32[]{:S(2)}, u32[]{:S(2)}) collective-permute-start(bf16[32,13312]{1,0:T(8,128)(2,1)} %collective-permute-done.44.t2), channel_id=1, source_target_pairs={{0,1},{1,0},{2,3},{3,2},{4,5},{5,4},{6,7},{7,6},{8,9},{9,8},{10,11... | collective-permute-start | bytes 2555912 | tf_op jit(solution)/shard_map/ppermute | solution.py:18
  379.0 25.7 %collective-permute-start.41 = (bf16[128,512]{1,0:T(8,128)(2,1)S(1)}, bf16[128,512]{1,0:T(8,128)(2,1)S(1)}, u32[]{:S(2)}, u32[]{:S(2)}) collective-permute-start(bf16[128,512]{1,0:T(8,128)(2,1)S(1)} %fusion.8), channel_id=1, source_target_pairs={{0,8},{4,12},{8,0},{12,4},{1,9},{5,13},{9,1},{13,5},{2,10},{6,14},... | collective-permute-start | bytes 393224 | tf_op jit(solution)/shard_map/ppermute | solution.py:18
  386.8 45.9 %collective-permute-start.56 = (bf16[16,13312]{1,0:T(8,128)(2,1)}, bf16[16,13312]{1,0:T(8,128)(2,1)S(1)}, u32[]{:S(2)}, u32[]{:S(2)}) collective-permute-start(bf16[16,13312]{1,0:T(8,128)(2,1)} %get-tuple-element.48.a_ref), channel_id=1, source_target_pairs={{4,8},{8,4},{5,9},{9,5},{6,10},{10,6},{7,11},{11,7},{20,24},{24,20... | collective-permute-start | bytes 1277960 | tf_op jit(solution)/shard_map/ppermute | solution.py:156
  387.5 54.1 %collective-permute-start.57 = (bf16[16,13312]{1,0:T(8,128)(2,1)}, bf16[16,13312]{1,0:T(8,128)(2,1)}, u32[]{:S(2)}, u32[]{:S(2)}) collective-permute-start(bf16[16,13312]{1,0:T(8,128)(2,1)} %collective-permute-done.55.near_ref), channel_id=1, source_target_pairs={{4,8},{8,4},{5,9},{9,5},{6,10},{10,6},{7,11},{11,7},{20,24},{24,20... | collective-permute-start | bytes 1277960 | tf_op jit(solution)/shard_map/ppermute | solution.py:157
  404.7 36.6 %collective-permute-start.53 = (bf16[32,13312]{1,0:T(8,128)(2,1)S(1)}, bf16[32,13312]{1,0:T(8,128)(2,1)}, u32[]{:S(2)}, u32[]{:S(2)}) collective-permute-start(bf16[32,13312]{1,0:T(8,128)(2,1)S(1)} %broadcast_select_fusion.1.t0), channel_id=1, source_target_pairs={{0,2},{1,3},{2,0},{3,1},{4,6},{5,7},{6,4},{7,5},{8,10},{9,11},{10,... | collective-permute-start | bytes 2555912 | tf_op jit(solution)/shard_map/ppermute | solution.py:18
  407.9 51.2 %collective-permute-start.52 = (bf16[32,13312]{1,0:T(8,128)(2,1)S(1)}, bf16[32,13312]{1,0:T(8,128)(2,1)}, u32[]{:S(2)}, u32[]{:S(2)}) collective-permute-start(bf16[32,13312]{1,0:T(8,128)(2,1)S(1)} %broadcast_select_fusion.1.t0), channel_id=1, source_target_pairs={{0,1},{1,0},{2,3},{3,2},{4,5},{5,4},{6,7},{7,6},{8,9},{9,8},{10,11... | collective-permute-start | bytes 2555912 | tf_op jit(solution)/shard_map/ppermute | solution.py:18
  407.9 33.4 %collective-permute-start.60 = (bf16[32,13312]{1,0:T(8,128)(2,1)}, bf16[32,13312]{1,0:T(8,128)(2,1)S(1)}, u32[]{:S(2)}, u32[]{:S(2)}) collective-permute-start(bf16[32,13312]{1,0:T(8,128)(2,1)} %get-tuple-element.50), channel_id=1, source_target_pairs={{4,0},{8,12},{5,1},{9,13},{6,2},{10,14},{7,3},{11,15},{20,16},{24,... | collective-permute-start | bytes 2555912 | tf_op jit(solution)/shard_map/ppermute | solution.py:160
  432.8 18.2 %collective-permute-start.64 = (bf16[16,13312]{1,0:T(8,128)(2,1)}, bf16[16,13312]{1,0:T(8,128)(2,1)}, u32[]{:S(2)}, u32[]{:S(2)}) collective-permute-start(bf16[16,13312]{1,0:T(8,128)(2,1)} %get-tuple-element.51.a_ref), channel_id=1, source_target_pairs={{0,4},{12,8},{1,5},{13,9},{2,6},{14,10},{3,7},{15,11},{16,20},{28,... | collective-permute-start | bytes 1277960 | tf_op jit(solution)/shard_map/ppermute | solution.py:155
  441.2 15.6 %collective-permute-start.49 = (bf16[128,1024]{1,0:T(8,128)(2,1)S(1)}, bf16[128,1024]{1,0:T(8,128)(2,1)S(1)}, u32[]{:S(2)}, u32[]{:S(2)}) collective-permute-start(bf16[128,1024]{1,0:T(8,128)(2,1)S(1)} %pad_maximum_fusion.4), channel_id=1, source_target_pairs={{0,4},{4,0},{8,12},{12,8},{1,5},{5,1},{9,13},{13,9},{2,6},{6,2},{1... | collective-permute-start | bytes 786440 | tf_op jit(solution)/shard_map/ppermute | solution.py:18
  441.3 17.9 %collective-permute-start.54 = (bf16[32,13312]{1,0:T(8,128)(2,1)}, bf16[32,13312]{1,0:T(8,128)(2,1)}, u32[]{:S(2)}, u32[]{:S(2)}) collective-permute-start(bf16[32,13312]{1,0:T(8,128)(2,1)} %collective-permute-done.53.t2), channel_id=1, source_target_pairs={{0,1},{1,0},{2,3},{3,2},{4,5},{5,4},{6,7},{7,6},{8,9},{9,8},{10,11... | collective-permute-start | bytes 2555912 | tf_op jit(solution)/shard_map/ppermute | solution.py:18
  441.6 47.1 %collective-permute-start.65 = (bf16[16,13312]{1,0:T(8,128)(2,1)}, bf16[16,13312]{1,0:T(8,128)(2,1)}, u32[]{:S(2)}, u32[]{:S(2)}) collective-permute-start(bf16[16,13312]{1,0:T(8,128)(2,1)} %get-tuple-element.51.a_ref), channel_id=1, source_target_pairs={{4,8},{8,4},{5,9},{9,5},{6,10},{10,6},{7,11},{11,7},{20,24},{24,20... | collective-permute-start | bytes 1277960 | tf_op jit(solution)/shard_map/ppermute | solution.py:156
  450.9 38.2 %collective-permute-start.66 = (bf16[16,13312]{1,0:T(8,128)(2,1)}, bf16[16,13312]{1,0:T(8,128)(2,1)}, u32[]{:S(2)}, u32[]{:S(2)}) collective-permute-start(bf16[16,13312]{1,0:T(8,128)(2,1)} %collective-permute-done.64.near_ref), channel_id=1, source_target_pairs={{4,8},{8,4},{5,9},{9,5},{6,10},{10,6},{7,11},{11,7},{20,24},{24,20... | collective-permute-start | bytes 1277960 | tf_op jit(solution)/shard_map/ppermute | solution.py:157
  456.8 49.1 %collective-permute-start.62 = (bf16[32,13312]{1,0:T(8,128)(2,1)S(1)}, bf16[32,13312]{1,0:T(8,128)(2,1)}, u32[]{:S(2)}, u32[]{:S(2)}) collective-permute-start(bf16[32,13312]{1,0:T(8,128)(2,1)S(1)} %broadcast_select_fusion.t0), channel_id=1, source_target_pairs={{0,2},{1,3},{2,0},{3,1},{4,6},{5,7},{6,4},{7,5},{8,10},{9,11},{10,... | collective-permute-start | bytes 2555912 | tf_op jit(solution)/shard_map/ppermute | solution.py:18
  459.1 57.7 %collective-permute-start.61 = (bf16[32,13312]{1,0:T(8,128)(2,1)S(1)}, bf16[32,13312]{1,0:T(8,128)(2,1)}, u32[]{:S(2)}, u32[]{:S(2)}) collective-permute-start(bf16[32,13312]{1,0:T(8,128)(2,1)S(1)} %broadcast_select_fusion.t0), channel_id=1, source_target_pairs={{0,1},{1,0},{2,3},{3,2},{4,5},{5,4},{6,7},{7,6},{8,9},{9,8},{10,11... | collective-permute-start | bytes 2555912 | tf_op jit(solution)/shard_map/ppermute | solution.py:18
  459.1 25.4 %collective-permute-start.69 = (bf16[16,13312]{1,0:T(8,128)(2,1)}, bf16[16,13312]{1,0:T(8,128)(2,1)S(1)}, u32[]{:S(2)}, u32[]{:S(2)}) collective-permute-start(bf16[16,13312]{1,0:T(8,128)(2,1)} %get-tuple-element.53), channel_id=1, source_target_pairs={{4,0},{8,12},{5,1},{9,13},{6,2},{10,14},{7,3},{11,15},{20,16},{24,... | collective-permute-start | bytes 1277960 | tf_op jit(solution)/shard_map/ppermute | solution.py:160
  484.6 14.1 %collective-permute-start.58 = (bf16[128,1024]{1,0:T(8,128)(2,1)}, bf16[128,1024]{1,0:T(8,128)(2,1)S(1)}, u32[]{:S(2)}, u32[]{:S(2)}) collective-permute-start(bf16[128,1024]{1,0:T(8,128)(2,1)} %pad_maximum_fusion.5), channel_id=1, source_target_pairs={{0,4},{4,0},{8,12},{12,8},{1,5},{5,1},{9,13},{13,9},{2,6},{6,2},{1... | collective-permute-start | bytes 786440 | tf_op jit(solution)/shard_map/ppermute | solution.py:18
  489.2 16.7 %collective-permute-start.71 = (bf16[16,13312]{1,0:T(8,128)(2,1)S(1)}, bf16[16,13312]{1,0:T(8,128)(2,1)S(1)}, u32[]{:S(2)}, u32[]{:S(2)}) collective-permute-start(bf16[16,13312]{1,0:T(8,128)(2,1)S(1)} %broadcast_select_fusion.8.t0), channel_id=1, source_target_pairs={{0,2},{1,3},{2,0},{3,1},{4,6},{5,7},{6,4},{7,5},{8,10},{9,11},{10,... | collective-permute-start | bytes 1277960 | tf_op jit(solution)/shard_map/ppermute | solution.py:18
  498.7 16.5 %collective-permute-start.75 = (bf16[16,13312]{1,0:T(8,128)(2,1)}, bf16[16,13312]{1,0:T(8,128)(2,1)S(1)}, u32[]{:S(2)}, u32[]{:S(2)}) collective-permute-start(bf16[16,13312]{1,0:T(8,128)(2,1)} %get-tuple-element.54), channel_id=1, source_target_pairs={{4,0},{8,12},{5,1},{9,13},{6,2},{10,14},{7,3},{11,15},{20,16},{24,... | collective-permute-start | bytes 1277960 | tf_op jit(solution)/shard_map/ppermute | solution.py:160
  505.9 33.0 %collective-permute-start.70 = (bf16[16,13312]{1,0:T(8,128)(2,1)S(1)}, bf16[16,13312]{1,0:T(8,128)(2,1)S(1)}, u32[]{:S(2)}, u32[]{:S(2)}) collective-permute-start(bf16[16,13312]{1,0:T(8,128)(2,1)S(1)} %broadcast_select_fusion.8.t0), channel_id=1, source_target_pairs={{0,1},{1,0},{2,3},{3,2},{4,5},{5,4},{6,7},{7,6},{8,9},{9,8},{10,11... | collective-permute-start | bytes 1277960 | tf_op jit(solution)/shard_map/ppermute | solution.py:18
  505.9 33.0 %collective-permute-start.72 = (bf16[16,13312]{1,0:T(8,128)(2,1)S(1)}, bf16[16,13312]{1,0:T(8,128)(2,1)S(1)}, u32[]{:S(2)}, u32[]{:S(2)}) collective-permute-start(bf16[16,13312]{1,0:T(8,128)(2,1)S(1)} %collective-permute-done.71.t2), channel_id=1, source_target_pairs={{0,1},{1,0},{2,3},{3,2},{4,5},{5,4},{6,7},{7,6},{8,9},{9,8},{10,11... | collective-permute-start | bytes 1277960 | tf_op jit(solution)/shard_map/ppermute | solution.py:18
  515.3 54.1 %collective-permute-start.77 = (bf16[16,13312]{1,0:T(8,128)(2,1)S(1)}, bf16[16,13312]{1,0:T(8,128)(2,1)S(1)}, u32[]{:S(2)}, u32[]{:S(2)}) collective-permute-start(bf16[16,13312]{1,0:T(8,128)(2,1)S(1)} %broadcast_select_fusion.7.t0), channel_id=1, source_target_pairs={{0,2},{1,3},{2,0},{3,1},{4,6},{5,7},{6,4},{7,5},{8,10},{9,11},{10,... | collective-permute-start | bytes 1277960 | tf_op jit(solution)/shard_map/ppermute | solution.py:18
  561.4 12.4 %collective-permute-start.67 = (bf16[128,1024]{1,0:T(8,128)(2,1)S(1)}, bf16[128,1024]{1,0:T(8,128)(2,1)S(1)}, u32[]{:S(2)}, u32[]{:S(2)}) collective-permute-start(bf16[128,1024]{1,0:T(8,128)(2,1)S(1)} %pad_maximum_fusion.6), channel_id=1, source_target_pairs={{0,4},{4,0},{8,12},{12,8},{1,5},{5,1},{9,13},{13,9},{2,6},{6,2},{1... | collective-permute-start | bytes 786440 | tf_op jit(solution)/shard_map/ppermute | solution.py:18
  573.9 24.9 %collective-permute-start.68 = (bf16[128,512]{1,0:T(8,128)(2,1)S(1)}, bf16[128,512]{1,0:T(8,128)(2,1)S(1)}, u32[]{:S(2)}, u32[]{:S(2)}) collective-permute-start(bf16[128,512]{1,0:T(8,128)(2,1)S(1)} %fusion.2), channel_id=1, source_target_pairs={{0,8},{4,12},{8,0},{12,4},{1,9},{5,13},{9,1},{13,5},{2,10},{6,14},... | collective-permute-start | bytes 393224 | tf_op jit(solution)/shard_map/ppermute | solution.py:18
  (48 other events, 713.1 us)
